TPU v7x, 256 devices: a whole 4x4x8 slice. The times are simulated.
256 devices in a mesh: cells: 128 (over x, z, y), harm: 2 (over core).
Axes of the slice: x: 4, y: 4, z: 8, core: 2. Of those that a mesh axis runs over, the one named last changes fastest.
Arguments:
- source: float32 [14, 4, 8192, 128], P('harm', None, 'cells'), may hold values from -6 to 6
- mode_shapes: bfloat16 [60, 8192, 128], P(None, 'cells'), may hold values from -5.4 to 5.4
- modal_real: float32 [7, 60, 60], replicated, may hold values from -2 to 9
- modal_imag: float32 [7, 60, 60], replicated, may hold values from -1 to 3
- harmonic_freq: float32 [7], replicated, may hold values from 0.2 to 1.5
- blade_of_row: int32 [8192], P('cells'), may hold values from 0 to 23, as said below
Outputs:
- wall_sensitivity: float32 [8192, 128], P(('cells', 'harm'))
- blade_load: float32 [24], replicated
Inputs may be any that keep to these rules, and one draw needn't show every extreme that they name: `blade_of_row`: never falls along the stations; every blade owns at least 170 consecutive stations.
All inputs are finite; a program needn't handle non-finite values.
Results may differ from a plain program's by a relative error of at most 0.0049.
Values sent between devices are 32-bit elements; how exact they have to be, the bound alone decides.
A program may use at most 64 MiB of HBM per device.

v0:
```python
import math

import jax
import jax.numpy as jnp
from jax import lax
from jax.sharding import PartitionSpec as P

BLADES = 24
STEPS = 3


RELAX = 0.15
DAMPING = 0.5


def from_partner(block, axis, stride):
    count = lax.axis_size(axis)
    route = []
    for low in range(count):
        high = low | 1 << stride
        if high != low and high < count:
            route += [(low, high), (high, low)]
    return lax.ppermute(block, axis, route)


def padded_2(shard, sides, width):
    for axis, dim in sides:
        devices, length = (lax.axis_size(axis), shard.shape[dim])
        up = [(i, (i + 1) % devices) for i in range(devices)]
        down = [(j, i) for i, j in up]
        last = lax.slice_in_dim(shard, length - width, length, axis=dim)
        initial = lax.slice_in_dim(shard, 0, width, axis=dim)
        before = lax.ppermute(last, axis, up)
        after = lax.ppermute(initial, axis, down)
        shard = jnp.concatenate([before, shard, after], axis=dim)
    return shard


def advance(center, upper, lower, partner_field, forcing, coupling):
    zero_chord = jnp.zeros_like(center[..., :1])
    right = jnp.concatenate([center[..., 1:], zero_chord], axis=-1)
    left = jnp.concatenate([zero_chord, center[..., :-1]], axis=-1)
    zero_layer = jnp.zeros_like(center[:, :1])
    deeper = jnp.concatenate([center[:, 1:], zero_layer], axis=1)
    higher = jnp.concatenate([zero_layer, center[:, :-1]], axis=1)
    laplace = upper + lower + right + left + deeper + higher - 6.0 * center
    return center + RELAX * (
        laplace - DAMPING * center + coupling[:, None, None, None] * partner_field + forcing
    )


def modal_solve(load, modal_real, modal_imag):
    harm_count = modal_real.shape[0]
    mode_count = modal_real.shape[1]
    top_rows = jnp.concatenate([modal_real, -modal_imag], axis=2)
    low_rows = jnp.concatenate([modal_imag, modal_real], axis=2)
    system = jnp.concatenate([top_rows, low_rows], axis=1)
    rhs = jnp.concatenate([load[:harm_count], load[harm_count:]], axis=1)
    normal = jnp.einsum("hji,hjk->hik", system, system, precision=lax.Precision.HIGHEST)
    moved = jnp.einsum("hji,hj->hi", system, rhs, precision=lax.Precision.HIGHEST)
    factor = jnp.linalg.cholesky(normal)
    solved = jax.vmap(
        lambda factor_one, vector_one: jax.scipy.linalg.cho_solve((factor_one, True), vector_one)
    )(factor, moved)
    return jnp.concatenate([solved[:, :mode_count], solved[:, mode_count:]], axis=0)


def swap_parts(field):
    return from_partner(field, "harm", 0)


def per_device(source, mode_shapes, modal_real, modal_imag, harmonic_freq, blade_of_row):
    harm_count = harmonic_freq.shape[0]
    half_index = lax.axis_index("harm")
    row_count = source.shape[2]
    chord_count = source.shape[3]
    half_rows = row_count // 2
    face_count = row_count * chord_count * lax.axis_size("cells")
    orient = 1.0 - 2.0 * half_index.astype(jnp.float32)
    coupling = orient * harmonic_freq
    field = source
    for step_index in range(STEPS):
        padded = padded_2(field, (("cells", 2),), 1)
        partner_field = swap_parts(field)
        field = advance(field, padded[:, :, 2:], padded[:, :, :-2], partner_field, source, coupling)
    wall = field[:, 0].astype(jnp.bfloat16)
    flat_wall = wall.reshape(harm_count, -1)
    shapes = mode_shapes.reshape(mode_shapes.shape[0], -1)
    partial_load = lax.dot_general(
        flat_wall, shapes, (((1,), (1,)), ((), ())), preferred_element_type=jnp.float32
    )
    passage_total = lax.psum(partial_load, "cells")
    summed = lax.all_gather(passage_total, "harm", axis=0, tiled=True)
    load = summed * jnp.float32(1.0 / math.sqrt(face_count))
    amplitudes = modal_solve(load, modal_real, modal_imag).astype(jnp.bfloat16)
    own_amplitudes = lax.dynamic_slice_in_dim(amplitudes, half_index * harm_count, harm_count, 0)
    rebuilt = jnp.dot(own_amplitudes, shapes, preferred_element_type=jnp.float32)
    partial_sens = jnp.sum(flat_wall.astype(jnp.float32) * rebuilt, axis=0).reshape(
        row_count, chord_count
    )
    sensitivity = lax.psum_scatter(partial_sens, "harm", scatter_dimension=0, tiled=True)
    own_blades = lax.dynamic_slice_in_dim(blade_of_row, half_index * half_rows, half_rows, 0)
    onehot = (own_blades[None, :] == jnp.arange(BLADES, dtype=jnp.int32)[:, None]).astype(
        jnp.float32
    )
    local_totals = jnp.dot(onehot, jnp.sum(sensitivity, axis=1), precision=lax.Precision.HIGHEST)
    local_counts = jnp.sum(onehot, axis=1) * chord_count
    totals, counts = lax.psum((local_totals, local_counts), ("cells", "harm"))
    return (sensitivity, totals * lax.rsqrt(counts))


def solution(mesh):
    placed = (P("harm", None, "cells", None), P(None, "cells", None), P(), P(), P(), P("cells"))
    return jax.shard_map(
        per_device,
        mesh=mesh,
        in_specs=placed,
        out_specs=(P(("cells", "harm"), None), P()),
        check_vma=False,
    )
```

profile of v0, /device:TPU:1, one launch (start us, length us, event | category | flops | bytes accessed | tf_op | source)
XLA Modules:
  0.0 642.7 jit_solution(1605088260689340853)
XLA Ops:
  7.2 3.3 collective-permute-start.2
  10.5 1.7 copy.60
  12.9 8.5 %collective-permute-start = (f32[7,4,1,128]{3,0,2,1:T(8,128)}, f32[7,4,1,128]{3,0,2,1:T(8,128)S(1)}, u32[]{:S(2)}, u32[]{:S(2)}) collective-permute-start(f32[7,4,1,128]{3,0,2,1:T(8,128)} %get-tuple-element.22), channel_id=1, source_target_pairs={{2,0},{4,2},{6,4},{8,6},{10,8},{12,10},{14,12},{16,14},{18,16},{20... | collective-permute-start | bytes 43016 | tf_op jit(solution)/shard_map/ppermute | solution.py:34
  21.5 0.7 copy-done.6
  22.5 1.2 fusion.42
  23.9 77.0 %custom-call.11 = f32[7,120,120]{2,1,0:T(8,128)S(1)} custom-call(f32[7,120,120]{2,1,0:T(8,128)S(1)} %fusion.33), custom_call_target="Cholesky" | custom-call | tf_op jit(solution)/shard_map/jit(cholesky)/cholesky | solution.py:61
  101.3 1.3 fusion.62
  102.5 1.6 fusion.61
  104.2 64.5 %custom-call.12 = f32[7,1,120,120]{2,3,1,0:T(8,128)S(1)} custom-call(f32[7,1,120,120]{3,2,1,0:T(8,128)S(1)} %select_bitcast_fusion), custom_call_target="InvertDiagBlocksLowerTriangular" | custom-call | tf_op jit(solution)/shard_map/vmap(jit(_cho_solve))/triangular_solve | solution.py:63
  168.8 0.7 copy.78
  170.3 3.3 fusion.27
  174.3 7.2 %collective-permute-start.3 = (f32[7,4,1,128]{3,0,2,1:T(8,128)S(1)}, f32[7,4,1,128]{3,0,2,1:T(8,128)S(1)}, u32[]{:S(2)}, u32[]{:S(2)}) collective-permute-start(f32[7,4,1,128]{3,0,2,1:T(8,128)S(1)} %get-tuple-element.12), channel_id=1, source_target_pairs={{2,0},{4,2},{6,4},{8,6},{10,8},{12,10},{14,12},{16,14},{18,16},{20... | collective-permute-start | bytes 43016 | tf_op jit(solution)/shard_map/ppermute | solution.py:34
  182.4 7.1 %collective-permute-done.4 = f32[7,4,1,128]{3,0,2,1:T(8,128)S(1)} collective-permute-done((f32[7,4,1,128]{3,0,2,1:T(8,128)S(1)}, f32[7,4,1,128]{3,0,2,1:T(8,128)S(1)}, u32[]{:S(2)}, u32[]{:S(2)}) %collective-permute-start.4) | collective-permute-done | bytes 14368 | tf_op jit(solution)/shard_map/ppermute | solution.py:33
  189.6 1.8 broadcast_multiply_fusion
  191.6 1.5 collective-permute-start.8
  193.1 1.5 collective-permute-start.7
  195.7 5.4 collective-permute-done.7
  203.1 286.8 %psum.21 = f32[7,60]{1,0:T(8,128)S(1)} all-reduce(f32[7,60]{1,0:T(8,128)S(1)} %convolution_bitcast_fusion), channel_id=1, replica_groups=mesh['cells'=128,'harm'=2] {'cells'}, use_global_device_ids=true, to_apply=%region_2.3 | all-reduce | flops 420 | bytes 3360 | tf_op jit(solution)/shard_map/psum | solution.py:92
  490.0 58.1 %all-gather = f32[2,7,60]{2,1,0:T(8,128)S(1)} all-gather(f32[1,7,60]{2,1,0:T(8,128)S(1)} %bitcast.51), channel_id=1, replica_groups=mesh['cells'=128,'harm'=2] {'harm'}, dimensions={0}, use_global_device_ids=true | all-gather | bytes 5040 | tf_op jit(solution)/shard_map/all_gather | solution.py:93
  549.2 0.8 fusion.29
  550.2 0.9 fusion
  551.1 6.0 reduce-scatter.2.cloned.1.call-done
  557.0 0.8 reduce_sum.28
  558.0 77.4 %all-reduce.12 = (f32[24]{0:T(128)S(1)}, f32[24]{0:T(128)S(1)}) all-reduce(f32[24]{0:T(128)S(1)} %convolution_bitcast_fusion.1, f32[24]{0:T(128)S(1)} %broadcast_multiply_fusion.2), channel_id=1, replica_groups=mesh['cells'=128,'harm'=2] {'cells','harm'}, use_global_device_ids=true, to_apply=%region_6.7 | all-reduce | flops 48 | bytes 384 | tf_op jit(solution)/shard_map/psum | solution.py:108
  (73 shorter events, 9.1 us)
Async XLA Ops:
  7.2 549.9 %reduce-scatter.2.cloned.1.call-start = ((), (), s32[]{:S(2)}) async-start(), calls=%async_computation.1 | async-start | bytes 49152 | tf_op jit(solution)/shard_map/reduce_scatter | solution.py:101
  7.2 163.0 %collective-permute-start.2 = (f32[7,4,64,128]{3,2,1,0:T(8,128)}, f32[7,4,64,128]{3,2,1,0:T(8,128)}, u32[]{:S(2)}, u32[]{:S(2)}) collective-permute-start(f32[7,4,64,128]{3,2,1,0:T(8,128)} %param.6), channel_id=1, source_target_pairs={{0,1},{1,0},{2,3},{3,2},{4,5},{5,4},{6,7},{7,6},{8,9},{9,8},{10,11... | collective-permute-start | bytes 2752520 | tf_op jit(solution)/shard_map/ppermute | solution.py:23
  10.5 10.9 %copy-start.4 = (f32[7,60,60]{2,1,0:T(8,128)S(1)}, f32[7,60,60]{2,1,0:T(8,128)}, u32[]{:S(2)}) copy-start(f32[7,60,60]{2,1,0:T(8,128)} %param.9) | copy-start | bytes 302404
  12.9 157.3 %collective-permute-start = (f32[7,4,1,128]{3,0,2,1:T(8,128)}, f32[7,4,1,128]{3,0,2,1:T(8,128)S(1)}, u32[]{:S(2)}, u32[]{:S(2)}) collective-permute-start(f32[7,4,1,128]{3,0,2,1:T(8,128)} %get-tuple-element.22), channel_id=1, source_target_pairs={{2,0},{4,2},{6,4},{8,6},{10,8},{12,10},{14,12},{16,14},{18,16},{20... | collective-permute-start | bytes 43016 | tf_op jit(solution)/shard_map/ppermute | solution.py:34
  21.4 148.9 %collective-permute-start.1 = (f32[7,4,1,128]{3,0,2,1:T(8,128)}, f32[7,4,1,128]{3,0,2,1:T(8,128)S(1)}, u32[]{:S(2)}, u32[]{:S(2)}) collective-permute-start(f32[7,4,1,128]{3,0,2,1:T(8,128)} %get-tuple-element.23), channel_id=1, source_target_pairs={{0,2},{2,4},{4,6},{6,8},{8,10},{10,12},{12,14},{14,16},{16,18},{18... | collective-permute-start | bytes 43016 | tf_op jit(solution)/shard_map/ppermute | solution.py:33
  21.4 1.0 copy-start.8
  21.5 0.7 copy-start.6
  102.5 1.6 copy-start.10
  102.5 66.2 %copy-start = (bf16[60,64,128]{2,1,0:T(8,128)(2,1)S(1)}, bf16[60,64,128]{2,1,0:T(8,128)(2,1)}, u32[]{:S(2)}) copy-start(bf16[60,64,128]{2,1,0:T(8,128)(2,1)} %param.7) | copy-start | bytes 2949124
  169.5 0.7 copy-start.11
  173.8 15.8 %collective-permute-start.5 = (f32[7,4,64,128]{3,2,1,0:T(8,128)S(1)}, f32[7,4,64,128]{3,2,1,0:T(8,128)S(1)}, u32[]{:S(2)}, u32[]{:S(2)}) collective-permute-start(f32[7,4,64,128]{3,2,1,0:T(8,128)S(1)} %copy.61), channel_id=1, source_target_pairs={{0,1},{1,0},{2,3},{3,2},{4,5},{5,4},{6,7},{7,6},{8,9},{9,8},{10,11... | collective-permute-start | bytes 2752520 | tf_op jit(solution)/shard_map/ppermute | solution.py:23
  174.3 8.1 %collective-permute-start.3 = (f32[7,4,1,128]{3,0,2,1:T(8,128)S(1)}, f32[7,4,1,128]{3,0,2,1:T(8,128)S(1)}, u32[]{:S(2)}, u32[]{:S(2)}) collective-permute-start(f32[7,4,1,128]{3,0,2,1:T(8,128)S(1)} %get-tuple-element.12), channel_id=1, source_target_pairs={{2,0},{4,2},{6,4},{8,6},{10,8},{12,10},{14,12},{16,14},{18,16},{20... | collective-permute-start | bytes 43016 | tf_op jit(solution)/shard_map/ppermute | solution.py:34
  181.5 8.0 %collective-permute-start.4 = (f32[7,4,1,128]{3,0,2,1:T(8,128)S(1)}, f32[7,4,1,128]{3,0,2,1:T(8,128)S(1)}, u32[]{:S(2)}, u32[]{:S(2)}) collective-permute-start(f32[7,4,1,128]{3,0,2,1:T(8,128)S(1)} %get-tuple-element.13), channel_id=1, source_target_pairs={{0,2},{2,4},{4,6},{6,8},{8,10},{10,12},{12,14},{14,16},{16,18},{18... | collective-permute-start | bytes 43016 | tf_op jit(solution)/shard_map/ppermute | solution.py:33
  181.9 7.7 %copy-start.1 = (f32[7,4,64,128]{3,2,1,0:T(8,128)S(1)}, f32[7,4,64,128]{3,2,1,0:T(8,128)}, u32[]{:S(2)}) copy-start(f32[7,4,64,128]{3,2,1,0:T(8,128)} %param.6) | copy-start | bytes 2752516
  191.6 10.0 %collective-permute-start.8 = (f32[7,4,64,128]{3,2,1,0:T(8,128)S(1)}, f32[7,4,64,128]{3,2,1,0:T(8,128)S(1)}, u32[]{:S(2)}, u32[]{:S(2)}) collective-permute-start(f32[7,4,64,128]{3,2,1,0:T(8,128)S(1)} %copy.64), channel_id=1, source_target_pairs={{0,1},{1,0},{2,3},{3,2},{4,5},{5,4},{6,7},{7,6},{8,9},{9,8},{10,11... | collective-permute-start | bytes 2752520 | tf_op jit(solution)/shard_map/ppermute | solution.py:23
  193.1 2.6 collective-permute-start.6
  193.1 8.0 %collective-permute-start.7 = (f32[7,4,1,128]{3,0,2,1:T(8,128)S(1)}, f32[7,4,1,128]{3,0,2,1:T(8,128)S(1)}, u32[]{:S(2)}, u32[]{:S(2)}) collective-permute-start(f32[7,4,1,128]{3,0,2,1:T(8,128)S(1)} %get-tuple-element.11), channel_id=1, source_target_pairs={{0,2},{2,4},{4,6},{6,8},{8,10},{10,12},{12,14},{14,16},{16,18},{18... | collective-permute-start | bytes 43016 | tf_op jit(solution)/shard_map/ppermute | solution.py:33
  201.8 0.7 copy-start.2
  202.4 345.7 %copy-start.5 = (f32[7,60,60]{2,1,0:T(8,128)S(1)}, f32[7,60,60]{2,1,0:T(8,128)}, u32[]{:S(2)}) copy-start(f32[7,60,60]{2,1,0:T(8,128)} %param.9) | copy-start | bytes 302404
  202.4 345.7 %copy-start.7 = (f32[7,60,60]{2,1,0:T(8,128)S(1)}, f32[7,60,60]{2,1,0:T(8,128)}, u32[]{:S(2)}) copy-start(f32[7,60,60]{2,1,0:T(8,128)} %copy-done.6) | copy-start | bytes 302404
  202.4 345.7 %copy-start.9 = (f32[7,60,60]{2,1,0:T(8,128)S(1)}, f32[7,60,60]{2,1,0:T(8,128)}, u32[]{:S(2)}) copy-start(f32[7,60,60]{2,1,0:T(8,128)} %param.8) | copy-start | bytes 302404
  549.2 0.9 copy-start.3
Sparse Core Ops, SparseCore 0:
  551.2 5.7 reduce-scatter.1
where the time goes:
time: 643 us
  blocking collectives  422 us (66%)
  other arithmetic  149 us (23%)
  starting transfers between devices  22.5 us (3%)
  waiting for transfers between devices  19.6 us (3%)
  between operations  14.3 us (2%)
  local copies, waits for them, and re-layouts  10 us (2%)
    psum x1, blocking collectives, per_device(): passage_total = lax.psum(partial_load, 'cells')  287 us
    psum x1, blocking collectives, per_device(): totals, counts = lax.psum((local_totals, local_counts), ('cells', 'harm'))  77.4 us
    another operation x4, other arithmetic, modal_solve(): factor = jnp.linalg.cholesky(normal)  77.2 us
    another operation x3, other arithmetic, modal_solve(): jax.scipy.linalg.cho_solve((factor_one, True), vector_one)  64.6 us
    all_gather x1, blocking collectives, per_device(): summed = lax.all_gather(passage_total, 'harm', axis=0, tiled=True)  58.1 us
    ppermute x3, starting transfers between devices, padded_2(): after = lax.ppermute(initial, axis, down)  15.7 us
  transfers between devices with their start and end apart: 10, of which 5 were waited for; matrix products, arithmetic and copies ran while one was open for 23% of the time, Pallas kernels for 0%

commit v1 on v0

v1 whole, which is shorter than its diff:
```python
import itertools

import jax
import jax.numpy as jnp
from jax import lax
from jax.experimental import pallas as pl
from jax.experimental.pallas import tpu as pltpu
from jax.sharding import PartitionSpec as P

BLADES = 24
RELAX = 0.15
DAMPING = 0.5
CENTER = 1.0 - 6.0 * RELAX - RELAX * DAMPING

HARM = 7
MODES = 60
LAYERS = 4
CHORD = 128
OWN = 32
ROWS = 48
FIRST = 5
SPAN = 38
XN, ZN, YN = 4, 8, 4
MESH = pl.DeviceIdType.MESH
HIGHEST = lax.Precision.HIGHEST


def place():
    cell = lax.axis_index("cells")
    return cell // (ZN * YN), (cell // YN) % ZN, cell % YN, lax.axis_index("harm")


def cell_of(x, z, y):
    return (x * ZN + z) * YN + y


def kernel(
    freq_ref, blade_ref, source_ref, shapes_ref, real_ref, imag_ref,
    sens_ref, load_ref,
    stage, shapes_raw, shapes_wide, shapes_flat, first, second, third, wall, wall_low,
    pair, gauss, inverse, packed, send1, recv1, send2, recv2, send3, recv3,
    local_sem, send_sem, recv_sem,
):
    x, z, y, h = place()
    cell = lax.axis_index("cells")
    cells = XN * ZN * YN
    member = y * 2 + h
    plane = x * ZN + z
    up_cell = lax.rem(cell + 1, cells)
    down_cell = lax.rem(cell + cells - 1, cells)
    mine = jnp.minimum(member, HARM - 1)

    start = h * 29
    own_row = 8 - 3 * h
    own_copy = pltpu.make_async_copy(
        source_ref.at[:, :, pl.ds(start, 35), :],
        stage.at[pl.ds(h * 8, HARM), :, pl.ds(own_row, 35), :],
        local_sem.at[0],
    )
    own_copy.start()
    shape_copy = pltpu.make_async_copy(
        shapes_ref.at[:, pl.ds(pl.multiple_of(h * OWN, OWN), OWN), :],
        shapes_raw.at[pl.ds(0, MODES)],
        local_sem.at[1],
    )
    shape_copy.start()
    real_copy = pltpu.make_async_copy(real_ref.at[mine], pair.at[0], local_sem.at[2])
    imag_copy = pltpu.make_async_copy(imag_ref.at[mine], pair.at[1], local_sem.at[3])
    real_copy.start()
    imag_copy.start()

    group = [(a, b) for a, b in itertools.product(range(YN), range(2)) if (a, b) != (0, 0)]
    planes = [(a, b) for a, b in itertools.product(range(XN), range(ZN)) if (a, b) != (0, 0)]
    barrier = pltpu.get_barrier_semaphore()

    def greet(device):
        pl.semaphore_signal(barrier, inc=1, device_id=device, device_id_type=MESH)

    def group_device(dy, dh):
        return cell_of(x, z, lax.rem(y + dy, YN)), lax.rem(h + dh, 2)

    def plane_device(dx, dz):
        return cell_of(lax.rem(x + dx, XN), lax.rem(z + dz, ZN), y), h

    edge_cell = jnp.where(h == 0, down_cell, up_cell)
    greet((edge_cell, 0))
    greet((edge_cell, 1))
    for dy, dh in group:
        greet(group_device(dy, dh))
    for dx, dz in planes:
        greet(plane_device(dx, dz))
    pl.semaphore_wait(barrier, 2 + len(group) + len(planes))

    sibling = pltpu.make_async_remote_copy(
        src_ref=source_ref.at[:, :, pl.ds((1 - h) * 29, 35), :],
        dst_ref=stage.at[pl.ds(h * 8, HARM), :, pl.ds(FIRST + 3 * h, 35), :],
        send_sem=send_sem.at[0],
        recv_sem=recv_sem.at[0],
        device_id=(cell, 1 - h),
        device_id_type=MESH,
    )
    high_edge = pltpu.make_async_remote_copy(
        src_ref=source_ref.at[:, pl.ds(0, 3), pl.ds(61, 3), :],
        dst_ref=stage.at[pl.ds(h * 8, HARM), pl.ds(0, 3), pl.ds(FIRST, 3), :],
        send_sem=send_sem.at[1],
        recv_sem=recv_sem.at[1 + h],
        device_id=(up_cell, 0),
        device_id_type=MESH,
    )
    low_edge = pltpu.make_async_remote_copy(
        src_ref=source_ref.at[:, pl.ds(0, 3), pl.ds(0, 3), :],
        dst_ref=stage.at[pl.ds(h * 8, HARM), pl.ds(0, 3), pl.ds(FIRST + 35, 3), :],
        send_sem=send_sem.at[2],
        recv_sem=recv_sem.at[1 + h],
        device_id=(down_cell, 1),
        device_id_type=MESH,
    )
    high_edge.start()
    low_edge.start()
    sibling.start()

    zero = jnp.zeros((ROWS, CHORD), jnp.float32)
    for layer in range(LAYERS):
        stage[7, layer] = zero
        stage[15, layer] = zero
    shapes_wide[pl.ds(MODES * OWN, 4 * OWN), :] = jnp.zeros((4 * OWN, CHORD), jnp.float32)

    shape_copy.wait()

    def widen(m, carry):
        shapes_wide[pl.ds(pl.multiple_of(m * OWN, OWN), OWN), :] = shapes_raw[m].astype(jnp.float32)
        return carry

    lax.fori_loop(0, MODES, widen, 0, unroll=4)

    def flatten(s, carry):
        rows = shapes_wide[pl.ds(s, 64, stride=OWN), :]
        shapes_flat[:, pl.ds(pl.multiple_of(s * CHORD, CHORD), CHORD)] = rows.astype(jnp.bfloat16)
        return carry

    lax.fori_loop(0, OWN, flatten, 0, unroll=4)

    lane = lax.broadcasted_iota(jnp.int32, (64, CHORD), 1)
    left_half = lane < 64
    real_copy.wait()
    imag_copy.wait()
    gauss[...] = jnp.zeros_like(gauss)
    gauss[0:MODES, 0:MODES] = pair[0]
    gauss[64 : 64 + MODES, 0:MODES] = pair[1]
    both = gauss[0:64, :] + pltpu.roll(gauss[64:128, :], 64, 1)
    system = jnp.concatenate([both, jnp.zeros_like(both)], axis=0)
    adjoint = jnp.transpose(system)
    gram = jnp.dot(adjoint, system, precision=HIGHEST, preferred_element_type=jnp.float32)
    top, low = gram[0:64], gram[64:128]
    gauss[0:64, :] = jnp.where(
        left_half, top + pltpu.roll(low, 64, 1), pltpu.roll(adjoint[0:64], 64, 1)
    )
    gauss[64:128, :] = jnp.where(
        left_half, pltpu.roll(top, 64, 1) - low, -pltpu.roll(adjoint[64:128], 64, 1)
    )

    def pivot(k, carry):
        pick = jnp.full((8, CHORD), k, jnp.int32)
        row_re = jnp.broadcast_to(gauss[pl.ds(k, 1), :], (8, CHORD))
        row_im = jnp.broadcast_to(gauss[pl.ds(64 + k, 1), :], (8, CHORD))
        scale = 1.0 / jnp.take_along_axis(row_re, pick, axis=1)
        row_re = row_re * scale
        row_im = row_im * scale
        for block in range(8):
            here, there = pl.ds(8 * block, 8), pl.ds(64 + 8 * block, 8)
            old_re, old_im = gauss[here, :], gauss[there, :]
            col_re = jnp.take_along_axis(old_re, pick, axis=1)
            col_im = jnp.take_along_axis(old_im, pick, axis=1)
            gauss[here, :] = old_re - col_re * row_re + col_im * row_im
            gauss[there, :] = old_im - col_re * row_im - col_im * row_re
        gauss[pl.ds(k, 1), :] = row_re[0:1]
        gauss[pl.ds(64 + k, 1), :] = row_im[0:1]
        return carry

    sub = lax.broadcasted_iota(jnp.int32, (16, CHORD), 0)
    lane16 = lax.broadcasted_iota(jnp.int32, (16, CHORD), 1)
    coupling = jnp.zeros((16, CHORD), jnp.float32)
    for k in range(HARM):
        value = RELAX * freq_ref[k]
        coupling = jnp.where(sub == k, value, jnp.where(sub == 8 + k, -value, coupling))
    not_last = lane16 < CHORD - 1
    not_first = lane16 > 0

    own_copy.wait()
    sibling.wait_recv()
    edge_wait = pltpu.make_async_copy(
        stage.at[pl.ds(0, HARM), pl.ds(0, 3), pl.ds(FIRST, 3), :],
        stage.at[pl.ds(0, HARM), pl.ds(0, 3), pl.ds(FIRST, 3), :],
        recv_sem.at[1],
    )
    edge_wait2 = pltpu.make_async_copy(
        stage.at[pl.ds(0, HARM), pl.ds(0, 3), pl.ds(FIRST, 3), :],
        stage.at[pl.ds(0, HARM), pl.ds(0, 3), pl.ds(FIRST, 3), :],
        recv_sem.at[2],
    )
    edge_wait.wait()
    edge_wait2.wait()

    flat_stage = stage.reshape(16 * LAYERS * ROWS, CHORD)

    def gather(t, carry):
        for layer in range(LAYERS):
            for part in range(2):
                row = part * 8 * LAYERS * ROWS + layer * ROWS + FIRST + t
                first[layer, t, pl.ds(8 * part, 8), :] = flat_stage[
                    pl.ds(row, 8, stride=LAYERS * ROWS), :
                ]
        return carry

    lax.fori_loop(0, SPAN, gather, 0, unroll=2)

    def relaxed(field, layers, layer, t):
        centre = field[layer, t]
        near = field[layer, t + 1] + field[layer, t - 1]
        near = near + jnp.where(not_last, pltpu.roll(centre, CHORD - 1, 1), 0.0)
        near = near + jnp.where(not_first, pltpu.roll(centre, 1, 1), 0.0)
        if layer + 1 < layers:
            near = near + field[layer + 1, t]
        if layer > 0:
            near = near + field[layer - 1, t]
        partner = jnp.concatenate([centre[8:16], centre[0:8]], axis=0)
        return CENTER * centre + coupling * partner + RELAX * (near + first[layer, t])

    def step_one(t, carry):
        for layer in range(3):
            second[layer, t] = relaxed(first, 4, layer, t)
        return carry

    def step_two(t, carry):
        for layer in range(2):
            third[layer, t] = relaxed(second, 3, layer, t)
        return carry

    lax.fori_loop(1, SPAN - 1, step_one, 0, unroll=2)
    lax.fori_loop(2, SPAN - 2, step_two, 0, unroll=2)

    blade_row = h * OWN
    low_blade = blade_ref[blade_row]
    high_blade = blade_ref[blade_row + OWN - 1]
    low_count = jnp.float32(0.0)
    for s in range(OWN):
        value = relaxed(third, 2, 0, s + 3).astype(jnp.bfloat16)
        weight = jnp.where(blade_ref[blade_row + s] == low_blade, jnp.float32(1.0), jnp.float32(0.0))
        low_count = low_count + weight
        wall[:, s * CHORD : (s + 1) * CHORD] = value
        wall_low[:, s * CHORD : (s + 1) * CHORD] = (value.astype(jnp.float32) * weight).astype(
            jnp.bfloat16
        )

    contract = (((1,), (1,)), ((), ()))
    packed[...] = jnp.zeros_like(packed)
    packed[0:16, 0:64] = lax.dot_general(
        wall[...], shapes_flat[...], contract, preferred_element_type=jnp.float32
    )
    packed[16:32, 0:64] = lax.dot_general(
        wall_low[...], shapes_flat[...], contract, preferred_element_type=jnp.float32
    )
    lane8 = lax.broadcasted_iota(jnp.int32, (8, CHORD), 1)
    whole = packed[0:8, :] + pltpu.roll(packed[8:16, :], 64, 1)
    lower = packed[16:24, :] + pltpu.roll(packed[24:32, :], 64, 1)
    upper = whole - lower
    lower = jnp.where(lane8 == 62, low_count, lower)
    upper = jnp.where(lane8 == 62, OWN - low_count, upper)
    low_id = jnp.full((1, CHORD), low_blade, jnp.int32).astype(jnp.float32)
    high_id = jnp.full((1, CHORD), high_blade, jnp.int32).astype(jnp.float32)
    for j in range(8):
        send1[j, 0:1, :] = lower[j : j + 1]
        send1[j, 1:2, :] = upper[j : j + 1]
        send1[j, 2:3, :] = low_id
        send1[j, 3:4, :] = high_id
    recv1[member] = send1[member]
    copies1 = []
    for dy, dh in group:
        to_cell, to_core = group_device(dy, dh)
        copy = pltpu.make_async_remote_copy(
            src_ref=send1.at[lax.rem(y + dy, YN) * 2 + to_core],
            dst_ref=recv1.at[member],
            send_sem=send_sem.at[3],
            recv_sem=recv_sem.at[3],
            device_id=(to_cell, to_core),
            device_id_type=MESH,
        )
        copy.start()
    all1 = pltpu.make_async_copy(recv1.at[pl.ds(0, 7)], recv1.at[pl.ds(0, 7)], recv_sem.at[3])
    lax.fori_loop(0, 20, pivot, 0)
    all1.wait()

    base = recv1[0, 2:3, :]
    sums = [jnp.zeros((1, CHORD), jnp.float32) for _ in range(3)]
    for j in range(8):
        for part in range(2):
            row = recv1[j, part : part + 1, :]
            blade = recv1[j, 2 + part : 3 + part, :] - base
            for r in range(3):
                sums[r] = sums[r] + jnp.where(blade == float(r), row, 0.0)
    for r in range(3):
        send2[r : r + 1, :] = sums[r]
    send2[3:4, :] = base
    recv2[plane] = send2[...]
    for dx, dz in planes:
        copy = pltpu.make_async_remote_copy(
            src_ref=send2,
            dst_ref=recv2.at[plane],
            send_sem=send_sem.at[4],
            recv_sem=recv_sem.at[4],
            device_id=plane_device(dx, dz),
            device_id_type=MESH,
        )
        copy.start()
    all2 = pltpu.make_async_copy(recv2.at[pl.ds(0, 31)], recv2.at[pl.ds(0, 31)], recv_sem.at[4])

    lax.fori_loop(20, MODES, pivot, 0)
    back_re = pltpu.roll(gauss[0:64, :], 64, 1)
    back_im = pltpu.roll(gauss[64:128, :], 64, 1)
    inverse[0:64, :] = jnp.where(left_half, back_re, -gauss[64:128, :])
    inverse[64:128, :] = jnp.where(left_half, back_im, gauss[0:64, :])

    all2.wait()
    everything = recv2[...]
    summed = jnp.sum(everything, axis=0)
    total = summed[0:1] + summed[1:2] + summed[2:3]
    lane1 = lax.broadcasted_iota(jnp.int32, (1, CHORD), 1)
    used = (lane1 < MODES) | ((lane1 >= 64) & (lane1 < 64 + MODES))
    total = jnp.where(used, total * (1.0 / 1024.0), 0.0)
    solved = lax.dot_general(
        jnp.broadcast_to(total, (8, CHORD)), inverse[...], contract,
        precision=HIGHEST, preferred_element_type=jnp.float32,
    )[0:1]
    amplitude = jnp.where(used, solved, 0.0).astype(jnp.bfloat16).astype(jnp.float32)
    row3 = lax.broadcasted_iota(jnp.int32, (32, 4, CHORD), 1).astype(jnp.float32)
    lane3 = lax.broadcasted_iota(jnp.int32, (32, 4, CHORD), 2).astype(jnp.float32)
    belongs = (everything[:, 3:4, :] + row3 == lane3) & (row3 < 3.0)
    dots = jnp.sum(everything * amplitude, axis=2, keepdims=True)
    shares = jnp.sum(jnp.sum(jnp.where(belongs, dots, 0.0), axis=0), axis=0, keepdims=True)

    send3[0:1, :] = amplitude
    send3[1:2, :] = shares
    recv3[member] = send3[...]
    for dy, dh in group:
        copy = pltpu.make_async_remote_copy(
            src_ref=send3,
            dst_ref=recv3.at[member],
            send_sem=send_sem.at[5],
            recv_sem=recv_sem.at[5],
            device_id=group_device(dy, dh),
            device_id_type=MESH,
        )
        copy.start()
    all3 = pltpu.make_async_copy(recv3.at[pl.ds(0, 7)], recv3.at[pl.ds(0, 7)], recv_sem.at[5])

    counted = jnp.sum(jnp.where(lane3 == 62.0, everything, 0.0), axis=2, keepdims=True)
    counts = jnp.sum(jnp.sum(jnp.where(belongs, counted, 0.0), axis=0), axis=0, keepdims=True)
    counts = jnp.where(lane1 < BLADES, counts * CHORD, 1.0)
    all3.wait()

    totals = recv3[0, 1:2, :]
    for j in range(1, 8):
        totals = totals + recv3[j, 1:2, :]
    load_ref[...] = totals * lax.rsqrt(counts)
    amplitudes = jnp.concatenate([recv3[j, 0:1, :] for j in range(8)], axis=0)
    both_parts = jnp.concatenate([amplitudes, pltpu.roll(amplitudes, 64, 1)], axis=0)
    both_parts = both_parts[:, 0:64].astype(jnp.bfloat16)
    for s in range(0, OWN, 4):
        lanes = slice(s * CHORD, (s + 4) * CHORD)
        rebuilt = jnp.dot(both_parts, shapes_flat[:, lanes], preferred_element_type=jnp.float32)
        product = jnp.sum(rebuilt * wall[:, lanes].astype(jnp.float32), axis=0, keepdims=True)
        for i in range(4):
            sens_ref[s + i : s + i + 1, :] = product[:, i * CHORD : (i + 1) * CHORD]

    sibling.wait_send()
    high_edge.wait_send()
    low_edge.wait_send()
    pltpu.make_async_copy(recv1.at[pl.ds(0, 7)], recv1.at[pl.ds(0, 7)], send_sem.at[3]).wait()
    pltpu.make_async_copy(recv2.at[pl.ds(0, 31)], recv2.at[pl.ds(0, 31)], send_sem.at[4]).wait()
    pltpu.make_async_copy(recv3.at[pl.ds(0, 7)], recv3.at[pl.ds(0, 7)], send_sem.at[5]).wait()


def per_device(source, mode_shapes, modal_real, modal_imag, harmonic_freq, blade_of_row):
    f32, bf16 = jnp.float32, jnp.bfloat16
    any_space = pl.BlockSpec(memory_space=pl.ANY)
    smem = pl.BlockSpec(memory_space=pltpu.SMEM)
    vmem = pl.BlockSpec(memory_space=pltpu.VMEM)
    sens, load = pl.pallas_call(
        kernel,
        name="flutter",
        out_shape=(
            jax.ShapeDtypeStruct((OWN, CHORD), f32),
            jax.ShapeDtypeStruct((1, CHORD), f32),
        ),
        in_specs=[smem, smem, any_space, any_space, any_space, any_space],
        out_specs=(vmem, vmem),
        scratch_shapes=[
            pltpu.VMEM((16, LAYERS, ROWS, CHORD), f32),
            pltpu.VMEM((MODES, OWN, CHORD), bf16),
            pltpu.VMEM((64 * OWN, CHORD), f32),
            pltpu.VMEM((64, OWN * CHORD), bf16),
            pltpu.VMEM((LAYERS, SPAN, 16, CHORD), f32),
            pltpu.VMEM((3, SPAN, 16, CHORD), f32),
            pltpu.VMEM((2, SPAN, 16, CHORD), f32),
            pltpu.VMEM((16, OWN * CHORD), bf16),
            pltpu.VMEM((16, OWN * CHORD), bf16),
            pltpu.VMEM((2, MODES, MODES), f32),
            pltpu.VMEM((CHORD, CHORD), f32),
            pltpu.VMEM((CHORD, CHORD), f32),
            pltpu.VMEM((32, CHORD), f32),
            pltpu.VMEM((8, 4, CHORD), f32),
            pltpu.VMEM((8, 4, CHORD), f32),
            pltpu.VMEM((4, CHORD), f32),
            pltpu.VMEM((32, 4, CHORD), f32),
            pltpu.VMEM((2, CHORD), f32),
            pltpu.VMEM((8, 2, CHORD), f32),
            pltpu.SemaphoreType.DMA((4,)),
            pltpu.SemaphoreType.DMA((6,)),
            pltpu.SemaphoreType.DMA((6,)),
        ],
        compiler_params=pltpu.CompilerParams(
            collective_id=0, has_side_effects=True, vmem_limit_bytes=24 * 1024 * 1024
        ),
    )(harmonic_freq, blade_of_row, source, mode_shapes, modal_real, modal_imag)
    return sens, load[0, :BLADES]


def solution(mesh):
    placed = (P("harm", None, "cells", None), P(None, "cells", None), P(), P(), P(), P("cells"))
    return jax.shard_map(
        per_device,
        mesh=mesh,
        in_specs=placed,
        out_specs=(P(("cells", "harm"), None), P()),
        check_vma=False,
    )
```

time: 643 us -> 43.2 us (0.07)
  blocking collectives: 422 us -> 0 us
  other arithmetic: 149 us -> 0 us
  Pallas kernels: 0 us -> 35.6 us
  starting transfers between devices: 22.5 us -> 0 us
  waiting for transfers between devices: 19.6 us -> 0 us
  between operations: 14.3 us -> 0.65 us
    psum x2 -> x0, blocking collectives: 364 us -> none  [the longest x1 287 us: per_device(): passage_total = lax.psum(partial_load, 'cells')]
    another operation x7 -> x0, other arithmetic: 142 us -> none  [the longest x4 77.2 us: modal_solve(): factor = jnp.linalg.cholesky(normal)]
    all_gather x1 -> x0, blocking collectives: 58.1 us -> none  [per_device(): summed = lax.all_gather(passage_total, 'harm', axis=0, tiled=True)]
    pallas_call x0 -> x1, Pallas kernels: none -> 35.6 us  [per_device(): pl.pallas_call(kernel, name='flutter', out_shape=(jax.ShapeDtypeStruct((O...]
    ppermute x9 -> x0, starting transfers between devices: 22.5 us -> none  [the longest x3 15.7 us: padded_2(): after = lax.ppermute(initial, axis, down)]
    ppermute x9 -> x0, waiting for transfers between devices: 13.7 us -> none  [the longest x3 12.6 us: padded_2(): before = lax.ppermute(last, axis, up)]
  transfers between devices with their start and end apart: 10 -> 0, of which waited for: 5 -> 0; matrix products, arithmetic and copies ran while one was open for 23% -> 0% of each run, Pallas kernels for 0% -> 0%
where the time goes in v1:
time: 43.2 us; the launch traced here: 43 us
  Pallas kernels  35.6 us (82%)
  local copies, waits for them, and re-layouts  6.68 us (15%)
  between operations  0.65 us (2%)
    pallas_call x1, Pallas kernels, per_device(): pl.pallas_call(kernel, name='flutter', out_shape=(jax.ShapeDtypeStruct((O...  35.6 us
    unnamed x13, local copies, waits for them, and re-layouts  6.16 us

profile of v1, /device:TPU:1, one launch (start us, length us, event | category | flops | bytes accessed | tf_op | source)
XLA Modules:
  0.0 43.0 jit_solution(17899642996173217969)
XLA Ops:
  0.6 0.0 copy-start
  0.6 1.2 %copy-done = bf16[60,64,128]{2,1,0:T(8,128)(2,1)S(1)} copy-done((bf16[60,64,128]{2,1,0:T(8,128)(2,1)S(1)}, bf16[60,64,128]{2,1,0:T(8,128)(2,1)}, u32[]{:S(2)}) %copy-start) | copy-done | bytes 983064
  1.8 0.0 copy-start.1
  1.8 1.2 %copy-done.1 = f32[7,4,64,128]{3,2,1,0:T(8,128)S(1)} copy-done((f32[7,4,64,128]{3,2,1,0:T(8,128)S(1)}, f32[7,4,64,128]{3,2,1,0:T(8,128)}, u32[]{:S(2)}) %copy-start.1) | copy-done | bytes 917528
  3.0 0.0 copy-start.2
  3.0 0.9 %copy-done.2 = f32[7,60,60]{2,1,0:T(8,128)S(1)} copy-done((f32[7,60,60]{2,1,0:T(8,128)S(1)}, f32[7,60,60]{2,1,0:T(8,128)}, u32[]{:S(2)}) %copy-start.2) | copy-done | bytes 100824
  4.0 0.0 copy-start.3
  4.0 0.9 %copy-done.3 = f32[7,60,60]{2,1,0:T(8,128)S(1)} copy-done((f32[7,60,60]{2,1,0:T(8,128)S(1)}, f32[7,60,60]{2,1,0:T(8,128)}, u32[]{:S(2)}) %copy-start.3) | copy-done | bytes 100824
  4.9 0.0 copy-start.4
  4.9 0.7 %copy-done.4 = f32[7]{0:T(128)S(1)} copy-done((f32[7]{0:T(128)S(1)}, f32[7]{0:T(128)}, u32[]{:S(2)}) %copy-start.4) | copy-done | bytes 52
  5.5 0.0 copy-start.5
  5.5 0.7 %copy-done.5 = s32[64]{0:T(128)S(1)} copy-done((s32[64]{0:T(128)S(1)}, s32[64]{0:T(128)}, u32[]{:S(2)}) %copy-start.5) | copy-done | bytes 280
  6.2 35.6 %flutter.1 = (f32[32,128]{1,0:T(8,128)S(1)}, f32[1,128]{1,0:T(1,128)S(1)}) custom-call(f32[7]{0:T(128)S(1)} %copy-done.4, s32[64]{0:T(128)S(1)} %copy-done.5, f32[7,4,64,128]{3,2,1,0:T(8,128)S(1)} %copy-done.1, bf16[60,64,128]{2,1,0:T(8,128)(2,1)S(1)} %copy-done, f32[7,60,60]{2,1,0:T(8,128)S(1)} %copy-done.2, f32[7,60,60]{2,1,0:T(8,128)S(1)} %copy-done.3), custom_call_target="tpu_custom_call" | custom-call | tf_op jit(solution)/shard_map/flutter/pallas_call | solution.py:388
  41.9 0.5 %slice_bitcast_fusion = f32[24]{0:T(128)} fusion(f32[1,128]{1,0:T(1,128)S(1)} %get-tuple-element.5), kind=kLoop, calls=%fused_computation | loop fusion | bytes 192 | tf_op jit(solution)/shard_map/squeeze | solution.py:425
  42.4 0.6 %copy.9 = f32[32,128]{1,0:T(8,128)} copy(f32[32,128]{1,0:T(8,128)S(1)} %get-tuple-element.8) | data formatting | bytes 32768
Async XLA Ops:
  0.6 1.2 %copy-start = (bf16[60,64,128]{2,1,0:T(8,128)(2,1)S(1)}, bf16[60,64,128]{2,1,0:T(8,128)(2,1)}, u32[]{:S(2)}) copy-start(bf16[60,64,128]{2,1,0:T(8,128)(2,1)} %shapes_ref.1) | copy-start | bytes 2949124
  1.8 1.2 %copy-start.1 = (f32[7,4,64,128]{3,2,1,0:T(8,128)S(1)}, f32[7,4,64,128]{3,2,1,0:T(8,128)}, u32[]{:S(2)}) copy-start(f32[7,4,64,128]{3,2,1,0:T(8,128)} %source_ref.1) | copy-start | bytes 2752516
  3.0 0.9 %copy-start.2 = (f32[7,60,60]{2,1,0:T(8,128)S(1)}, f32[7,60,60]{2,1,0:T(8,128)}, u32[]{:S(2)}) copy-start(f32[7,60,60]{2,1,0:T(8,128)} %real_ref.1) | copy-start | bytes 302404
  4.0 0.9 %copy-start.3 = (f32[7,60,60]{2,1,0:T(8,128)S(1)}, f32[7,60,60]{2,1,0:T(8,128)}, u32[]{:S(2)}) copy-start(f32[7,60,60]{2,1,0:T(8,128)} %imag_ref.1) | copy-start | bytes 302404
  4.9 0.7 %copy-start.4 = (f32[7]{0:T(128)S(1)}, f32[7]{0:T(128)}, u32[]{:S(2)}) copy-start(f32[7]{0:T(128)} %freq_ref.1) | copy-start | bytes 88
  5.5 0.7 %copy-start.5 = (s32[64]{0:T(128)S(1)}, s32[64]{0:T(128)}, u32[]{:S(2)}) copy-start(s32[64]{0:T(128)} %blade_ref.1) | copy-start | bytes 772

commit v2 on v1

--- a/solution.py
+++ b/solution.py
@@ -35,11 +35,11 @@
 
 
 def kernel(
-    freq_ref, blade_ref, source_ref, shapes_ref, real_ref, imag_ref,
+    freq_hbm, blade_hbm, source_ref, shapes_ref, real_ref, imag_ref,
     sens_ref, load_ref,
     stage, shapes_raw, shapes_wide, shapes_flat, first, second, third, wall, wall_low,
     pair, gauss, inverse, packed, send1, recv1, send2, recv2, send3, recv3,
-    local_sem, send_sem, recv_sem,
+    freq_ref, blade_ref, local_sem, send_sem, recv_sem,
 ):
     x, z, y, h = place()
     cell = lax.axis_index("cells")
@@ -66,8 +66,12 @@
     shape_copy.start()
     real_copy = pltpu.make_async_copy(real_ref.at[mine], pair.at[0], local_sem.at[2])
     imag_copy = pltpu.make_async_copy(imag_ref.at[mine], pair.at[1], local_sem.at[3])
+    freq_copy = pltpu.make_async_copy(freq_hbm, freq_ref, local_sem.at[4])
+    blade_copy = pltpu.make_async_copy(blade_hbm, blade_ref, local_sem.at[5])
     real_copy.start()
     imag_copy.start()
+    freq_copy.start()
+    blade_copy.start()
 
     group = [(a, b) for a, b in itertools.product(range(YN), range(2)) if (a, b) != (0, 0)]
     planes = [(a, b) for a, b in itertools.product(range(XN), range(ZN)) if (a, b) != (0, 0)]
@@ -179,6 +183,8 @@
 
     sub = lax.broadcasted_iota(jnp.int32, (16, CHORD), 0)
     lane16 = lax.broadcasted_iota(jnp.int32, (16, CHORD), 1)
+    freq_copy.wait()
+    blade_copy.wait()
     coupling = jnp.zeros((16, CHORD), jnp.float32)
     for k in range(HARM):
         value = RELAX * freq_ref[k]
@@ -382,17 +388,17 @@
 
 def per_device(source, mode_shapes, modal_real, modal_imag, harmonic_freq, blade_of_row):
     f32, bf16 = jnp.float32, jnp.bfloat16
-    any_space = pl.BlockSpec(memory_space=pl.ANY)
-    smem = pl.BlockSpec(memory_space=pltpu.SMEM)
+    operands = (harmonic_freq, blade_of_row, source, mode_shapes, modal_real, modal_imag)
+    hbm = pl.BlockSpec(memory_space=pltpu.HBM)
     vmem = pl.BlockSpec(memory_space=pltpu.VMEM)
     sens, load = pl.pallas_call(
         kernel,
         name="flutter",
         out_shape=(
-            jax.ShapeDtypeStruct((OWN, CHORD), f32),
-            jax.ShapeDtypeStruct((1, CHORD), f32),
+            pltpu.VMEM((OWN, CHORD), f32),
+            pltpu.VMEM((1, CHORD), f32),
         ),
-        in_specs=[smem, smem, any_space, any_space, any_space, any_space],
+        in_specs=[hbm] * 6,
         out_specs=(vmem, vmem),
         scratch_shapes=[
             pltpu.VMEM((16, LAYERS, ROWS, CHORD), f32),
@@ -414,14 +420,16 @@
             pltpu.VMEM((32, 4, CHORD), f32),
             pltpu.VMEM((2, CHORD), f32),
             pltpu.VMEM((8, 2, CHORD), f32),
-            pltpu.SemaphoreType.DMA((4,)),
+            pltpu.SMEM((HARM,), f32),
+            pltpu.SMEM((2 * OWN,), jnp.int32),
+            pltpu.SemaphoreType.DMA((6,)),
             pltpu.SemaphoreType.DMA((6,)),
             pltpu.SemaphoreType.DMA((6,)),
         ],
         compiler_params=pltpu.CompilerParams(
-            collective_id=0, has_side_effects=True, vmem_limit_bytes=24 * 1024 * 1024
+            collective_id=0, has_side_effects=True, vmem_limit_bytes=32 * 1024 * 1024
         ),
-    )(harmonic_freq, blade_of_row, source, mode_shapes, modal_real, modal_imag)
+    )(*(pltpu.with_memory_space_constraint(a, pltpu.HBM) for a in operands))
     return sens, load[0, :BLADES]
 
 

time: 43.2 us -> 37.1 us (0.86)
  local copies, waits for them, and re-layouts: 6.68 us -> 1.12 us
    unnamed x13 -> x1, local copies, waits for them, and re-layouts: 6.16 us -> 0.61 us
where the time goes in v2:
time: 37.1 us
  Pallas kernels  35.3 us (95%)
  local copies, waits for them, and re-layouts  1.12 us (3%)
  between operations  0.64 us (2%)
    pallas_call x1, Pallas kernels, per_device(): pl.pallas_call(kernel, name='flutter', out_shape=(pltpu.VMEM((OWN, CHORD)...  35.3 us

profile of v2, /device:TPU:1, one launch (start us, length us, event | category | flops | bytes accessed | tf_op | source)
XLA Modules:
  0.0 37.1 jit_solution(15385672542142480739)
XLA Ops:
  0.6 35.3 %flutter.1 = (f32[32,128]{1,0:T(8,128)S(1)}, f32[1,128]{1,0:T(1,128)S(1)}) custom-call(f32[7]{0:T(128)} %freq_hbm.1, s32[64]{0:T(128)} %blade_hbm.1, f32[7,4,64,128]{3,2,1,0:T(8,128)} %source_ref.1, bf16[60,64,128]{2,1,0:T(8,128)(2,1)} %shapes_ref.1, f32[7,60,60]{2,1,0:T(8,128)} %real_ref.1, f32[7,60,60]{2,1,0:T(8,128)} %imag_ref.1), custom_call_target="tpu_custom_call" | custom-call | tf_op jit(solution)/shard_map/flutter/pallas_call | solution.py:394
  35.9 0.6 %copy.9 = f32[32,128]{1,0:T(8,128)} copy(f32[32,128]{1,0:T(8,128)S(1)} %get-tuple-element.6) | data formatting | bytes 32768
  36.5 0.5 %slice_bitcast_fusion = f32[24]{0:T(128)} fusion(f32[1,128]{1,0:T(1,128)S(1)} %get-tuple-element.5), kind=kLoop, calls=%fused_computation | loop fusion | bytes 192 | tf_op jit(solution)/shard_map/squeeze | solution.py:433

commit v3 on v2

v3 whole, which is shorter than its diff:
```python
import itertools

import jax
import jax.numpy as jnp
from jax import lax
from jax.experimental import pallas as pl
from jax.experimental.pallas import tpu as pltpu
from jax.sharding import PartitionSpec as P

BLADES = 24
RELAX = 0.15
DAMPING = 0.5
CENTER = 1.0 - 6.0 * RELAX - RELAX * DAMPING

HARM = 7
MODES = 60
LAYERS = 4
CHORD = 128
OWN = 32
SPAN = 38
XN, ZN, YN = 4, 8, 4
MESH = pl.DeviceIdType.MESH
HIGHEST = lax.Precision.HIGHEST


def place():
    cell = lax.axis_index("cells")
    return cell // (ZN * YN), (cell // YN) % ZN, cell % YN, lax.axis_index("harm")


def cell_of(x, z, y):
    return (x * ZN + z) * YN + y


def kernel(
    freq_hbm, blade_hbm, source_ref, shapes_ref, real_ref, imag_ref,
    sens_ref, load_ref,
    shapes_raw, shapes_wide, shapes_flat, first, second, third, wall, wall_low,
    pair, gauss, inverse, packed, send1, recv1, send2, recv2, send3, recv3,
    freq_ref, blade_ref, local_sem, send_sem, recv_sem, known_sem,
):
    x, z, y, h = place()
    cell = lax.axis_index("cells")
    cells = XN * ZN * YN
    member = y * 2 + h
    plane = x * ZN + z
    up_cell = lax.rem(cell + 1, cells)
    down_cell = lax.rem(cell + cells - 1, cells)
    mine = jnp.minimum(member, HARM - 1)

    group = [(a, b) for a, b in itertools.product(range(YN), range(2)) if (a, b) != (0, 0)]
    planes = [(a, b) for a, b in itertools.product(range(XN), range(ZN)) if (a, b) != (0, 0)]
    barrier = pltpu.get_barrier_semaphore()

    def group_device(dy, dh):
        return cell_of(x, z, lax.rem(y + dy, YN)), lax.rem(h + dh, 2)

    def plane_device(dx, dz):
        return cell_of(lax.rem(x + dx, XN), lax.rem(z + dz, ZN), y), h

    edge_cell = jnp.where(h == 0, down_cell, up_cell)
    nearby = [(edge_cell, 0), (edge_cell, 1)]
    nearby += [group_device(dy, dh) for dy, dh in group]
    nearby += [plane_device(dx, 0) for dx in range(1, XN)]
    nearby += [plane_device(0, dz) for dz in (1, 2, ZN - 2, ZN - 1)]
    for device in nearby:
        pl.semaphore_signal(barrier, inc=1, device_id=device, device_id_type=MESH)

    start = h * 29
    for c in range(HARM):
        pltpu.make_async_copy(
            source_ref.at[c, :, pl.ds(start, 35), :],
            first.at[:, pl.ds(3 - 3 * h, 35), h * 8 + c, :],
            local_sem.at[0],
        ).start()
    shape_copy = pltpu.make_async_copy(
        shapes_ref.at[:, pl.ds(pl.multiple_of(h * OWN, OWN), OWN), :],
        shapes_raw.at[pl.ds(0, MODES)],
        local_sem.at[1],
    )
    shape_copy.start()
    real_copy = pltpu.make_async_copy(real_ref.at[mine], pair.at[0], local_sem.at[2])
    imag_copy = pltpu.make_async_copy(imag_ref.at[mine], pair.at[1], local_sem.at[3])
    freq_copy = pltpu.make_async_copy(freq_hbm, freq_ref, local_sem.at[4])
    blade_copy = pltpu.make_async_copy(blade_hbm, blade_ref, local_sem.at[5])
    real_copy.start()
    imag_copy.start()
    freq_copy.start()
    blade_copy.start()
    pl.semaphore_wait(barrier, len(nearby))

    for c in range(HARM):
        pltpu.make_async_remote_copy(
            src_ref=source_ref.at[c, pl.ds(0, 3), pl.ds(61, 3), :],
            dst_ref=first.at[pl.ds(0, 3), pl.ds(0, 3), h * 8 + c, :],
            send_sem=send_sem.at[1],
            recv_sem=recv_sem.at[1],
            device_id=(up_cell, 0),
            device_id_type=MESH,
        ).start()
        pltpu.make_async_remote_copy(
            src_ref=source_ref.at[c, pl.ds(0, 3), pl.ds(0, 3), :],
            dst_ref=first.at[pl.ds(0, 3), pl.ds(35, 3), h * 8 + c, :],
            send_sem=send_sem.at[2],
            recv_sem=recv_sem.at[1],
            device_id=(down_cell, 1),
            device_id_type=MESH,
        ).start()
    for c in range(HARM):
        pltpu.make_async_remote_copy(
            src_ref=source_ref.at[c, :, pl.ds((1 - h) * 29, 35), :],
            dst_ref=first.at[:, pl.ds(3 * h, 35), h * 8 + c, :],
            send_sem=send_sem.at[0],
            recv_sem=recv_sem.at[0],
            device_id=(cell, 1 - h),
            device_id_type=MESH,
        ).start()

    def arrived(array, sem):
        pltpu.make_async_copy(array, array, sem).wait()

    for dz in (2, ZN - 2):
        pl.semaphore_signal(
            known_sem.at[0], inc=1, device_id=plane_device(0, dz), device_id_type=MESH
        )

    shapes_wide[pl.ds(MODES * OWN, 4 * OWN), :] = jnp.zeros((4 * OWN, CHORD), jnp.float32)

    shape_copy.wait()

    def widen(m, carry):
        shapes_wide[pl.ds(pl.multiple_of(m * OWN, OWN), OWN), :] = shapes_raw[m].astype(jnp.float32)
        return carry

    lax.fori_loop(0, MODES, widen, 0, unroll=4)

    def flatten(s, carry):
        rows = shapes_wide[pl.ds(s, 64, stride=OWN), :]
        shapes_flat[:, pl.ds(pl.multiple_of(s * CHORD, CHORD), CHORD)] = rows.astype(jnp.bfloat16)
        return carry

    lax.fori_loop(0, OWN, flatten, 0, unroll=4)

    pl.semaphore_wait(known_sem.at[0], 2)
    for dx in range(1, XN):
        pl.semaphore_signal(
            known_sem.at[1], inc=1, device_id=plane_device(dx, 0), device_id_type=MESH
        )

    sub = lax.broadcasted_iota(jnp.int32, (16, CHORD), 0)
    lane16 = lax.broadcasted_iota(jnp.int32, (16, CHORD), 1)
    freq_copy.wait()
    blade_copy.wait()
    coupling = jnp.zeros((16, CHORD), jnp.float32)
    for k in range(HARM):
        value = RELAX * freq_ref[k]
        coupling = jnp.where(sub == k, value, jnp.where(sub == 8 + k, -value, coupling))
    not_last = lane16 < CHORD - 1
    not_first = lane16 > 0

    def relaxed(field, layers, layer, t):
        centre = field[layer, t]
        near = field[layer, t + 1] + field[layer, t - 1]
        near = near + jnp.where(not_last, pltpu.roll(centre, CHORD - 1, 1), 0.0)
        near = near + jnp.where(not_first, pltpu.roll(centre, 1, 1), 0.0)
        if layer + 1 < layers:
            near = near + field[layer + 1, t]
        if layer > 0:
            near = near + field[layer - 1, t]
        partner = jnp.concatenate([centre[8:16], centre[0:8]], axis=0)
        return CENTER * centre + coupling * partner + RELAX * (near + first[layer, t])

    blade_row = h * OWN
    low_blade = blade_ref[blade_row]
    high_blade = blade_ref[blade_row + OWN - 1]
    low_count = jnp.float32(0.0)
    for s in range(OWN):
        same = blade_ref[blade_row + s] == low_blade
        low_count = low_count + jnp.where(same, jnp.float32(1.0), jnp.float32(0.0))
    in_use = (sub != 7) & (sub != 15)

    def relax_rows(first_t, second_t, third_t, first_n, second_n, third_n):
        def step_one(i, carry):
            for layer in range(3):
                second[layer, first_t + i] = relaxed(first, 4, layer, first_t + i)
            return carry

        def step_two(i, carry):
            for layer in range(2):
                third[layer, second_t + i] = relaxed(second, 3, layer, second_t + i)
            return carry

        def step_three(i, carry):
            s = third_t - 3 + i
            value = jnp.where(in_use, relaxed(third, 2, 0, third_t + i), 0.0).astype(jnp.bfloat16)
            same = blade_ref[blade_row + s] == low_blade
            weight = jnp.where(same, jnp.float32(1.0), jnp.float32(0.0))
            lanes = pl.ds(pl.multiple_of(s * CHORD, CHORD), CHORD)
            wall[:, lanes] = value
            wall_low[:, lanes] = (value.astype(jnp.float32) * weight).astype(jnp.bfloat16)
            return carry

        lax.fori_loop(0, first_n, step_one, 0, unroll=min(first_n, 11))
        lax.fori_loop(0, second_n, step_two, 0, unroll=min(second_n, 16))
        lax.fori_loop(0, third_n, step_three, 0, unroll=True)

    contract = (((1,), (1,)), ((), ()))

    def loads(lanes):
        shapes = shapes_flat[:, lanes]
        for row, part in ((0, wall), (16, wall_low)):
            packed[row : row + 16, 0:64] += lax.dot_general(
                part[:, lanes], shapes, contract, preferred_element_type=jnp.float32
            )

    edge_lanes = pl.ds(pl.multiple_of(h * (29 * CHORD), CHORD), 3 * CHORD)
    wall[:, edge_lanes] = jnp.zeros((16, 3 * CHORD), jnp.bfloat16)
    wall_low[:, edge_lanes] = jnp.zeros((16, 3 * CHORD), jnp.bfloat16)
    packed[...] = jnp.zeros_like(packed)
    halves = first.at[:, pl.ds(0, 35), pl.ds(0, HARM), :]
    arrived(halves, local_sem.at[0])
    arrived(halves, recv_sem.at[0])
    relax_rows(4 - 3 * h, 4 - 2 * h, 6 - 3 * h, 33, 32, 29)
    loads(pl.ds(0, OWN * CHORD))
    edges = first.at[pl.ds(0, 3), pl.ds(0, 6), pl.ds(0, HARM), :]
    arrived(edges, recv_sem.at[1])
    relax_rows(1 + 33 * h, 2 + 31 * h, 3 + 29 * h, 3, 3, 3)
    loads(edge_lanes)

    lane8 = lax.broadcasted_iota(jnp.int32, (8, CHORD), 1)
    whole = packed[0:8, :] + pltpu.roll(packed[8:16, :], 64, 1)
    lower = packed[16:24, :] + pltpu.roll(packed[24:32, :], 64, 1)
    upper = whole - lower
    lower = jnp.where(lane8 == 62, low_count, lower)
    upper = jnp.where(lane8 == 62, OWN - low_count, upper)
    low_id = jnp.full((1, CHORD), low_blade, jnp.int32).astype(jnp.float32)
    high_id = jnp.full((1, CHORD), high_blade, jnp.int32).astype(jnp.float32)
    for j in range(8):
        send1[j, 0:1, :] = lower[j : j + 1]
        send1[j, 1:2, :] = upper[j : j + 1]
        send1[j, 2:3, :] = low_id
        send1[j, 3:4, :] = high_id
    recv1[member] = send1[member]
    for dy, dh in group:
        to_cell, to_core = group_device(dy, dh)
        copy = pltpu.make_async_remote_copy(
            src_ref=send1.at[lax.rem(y + dy, YN) * 2 + to_core],
            dst_ref=recv1.at[member],
            send_sem=send_sem.at[3],
            recv_sem=recv_sem.at[3],
            device_id=(to_cell, to_core),
            device_id_type=MESH,
        )
        copy.start()

    lane = lax.broadcasted_iota(jnp.int32, (64, CHORD), 1)
    left_half = lane < 64
    real_copy.wait()
    imag_copy.wait()
    gauss[...] = jnp.zeros_like(gauss)
    gauss[0:MODES, 0:MODES] = pair[0]
    gauss[64 : 64 + MODES, 0:MODES] = pair[1]
    both = gauss[0:64, :] + pltpu.roll(gauss[64:128, :], 64, 1)
    system = jnp.concatenate([both, jnp.zeros_like(both)], axis=0)
    adjoint = jnp.transpose(system)
    gram = jnp.dot(adjoint, system, precision=HIGHEST, preferred_element_type=jnp.float32)
    top, low = gram[0:64], gram[64:128]
    gauss[0:64, :] = jnp.where(
        left_half, top + pltpu.roll(low, 64, 1), pltpu.roll(adjoint[0:64], 64, 1)
    )
    gauss[64:128, :] = jnp.where(
        left_half, pltpu.roll(top, 64, 1) - low, -pltpu.roll(adjoint[64:128], 64, 1)
    )

    def pivot(k, carry):
        pick = jnp.full((8, CHORD), k, jnp.int32)
        row_re = jnp.broadcast_to(gauss[pl.ds(k, 1), :], (8, CHORD))
        row_im = jnp.broadcast_to(gauss[pl.ds(64 + k, 1), :], (8, CHORD))
        scale = 1.0 / jnp.take_along_axis(row_re, pick, axis=1)
        row_re = row_re * scale
        row_im = row_im * scale
        for block in range(8):
            here, there = pl.ds(8 * block, 8), pl.ds(64 + 8 * block, 8)
            old_re, old_im = gauss[here, :], gauss[there, :]
            col_re = jnp.take_along_axis(old_re, pick, axis=1)
            col_im = jnp.take_along_axis(old_im, pick, axis=1)
            gauss[here, :] = old_re - col_re * row_re + col_im * row_im
            gauss[there, :] = old_im - col_re * row_im - col_im * row_re
        gauss[pl.ds(k, 1), :] = row_re[0:1]
        gauss[pl.ds(64 + k, 1), :] = row_im[0:1]
        return carry

    lax.fori_loop(0, 20, pivot, 0)
    arrived(recv1.at[pl.ds(0, 7)], recv_sem.at[3])

    base = recv1[0, 2:3, :]
    sums = [jnp.zeros((1, CHORD), jnp.float32) for _ in range(3)]
    for j in range(8):
        for part in range(2):
            row = recv1[j, part : part + 1, :]
            blade = recv1[j, 2 + part : 3 + part, :] - base
            for r in range(3):
                sums[r] = sums[r] + jnp.where(blade == float(r), row, 0.0)
    for r in range(3):
        send2[r : r + 1, :] = sums[r]
    send2[3:4, :] = base
    recv2[plane] = send2[...]
    pl.semaphore_wait(known_sem.at[1], XN - 1)
    for dx, dz in planes:
        copy = pltpu.make_async_remote_copy(
            src_ref=send2,
            dst_ref=recv2.at[plane],
            send_sem=send_sem.at[4],
            recv_sem=recv_sem.at[4],
            device_id=plane_device(dx, dz),
            device_id_type=MESH,
        )
        copy.start()

    lax.fori_loop(20, MODES, pivot, 0)
    back_re = pltpu.roll(gauss[0:64, :], 64, 1)
    back_im = pltpu.roll(gauss[64:128, :], 64, 1)
    inverse[0:64, :] = jnp.where(left_half, back_re, -gauss[64:128, :])
    inverse[64:128, :] = jnp.where(left_half, back_im, gauss[0:64, :])

    arrived(recv2.at[pl.ds(0, 31)], recv_sem.at[4])
    everything = recv2[...]
    summed = jnp.sum(everything, axis=0)
    total = summed[0:1] + summed[1:2] + summed[2:3]
    lane1 = lax.broadcasted_iota(jnp.int32, (1, CHORD), 1)
    used = (lane1 < MODES) | ((lane1 >= 64) & (lane1 < 64 + MODES))
    total = jnp.where(used, total * (1.0 / 1024.0), 0.0)
    solved = lax.dot_general(
        jnp.broadcast_to(total, (8, CHORD)), inverse[...], contract,
        precision=HIGHEST, preferred_element_type=jnp.float32,
    )[0:1]
    amplitude = jnp.where(used, solved, 0.0).astype(jnp.bfloat16).astype(jnp.float32)

    def share(part):
        recv3[part, member] = send3[part]
        for dy, dh in group:
            pltpu.make_async_remote_copy(
                src_ref=send3.at[part],
                dst_ref=recv3.at[part, member],
                send_sem=send_sem.at[5 + part],
                recv_sem=recv_sem.at[5 + part],
                device_id=group_device(dy, dh),
                device_id_type=MESH,
            ).start()

    send3[0] = amplitude
    share(0)
    row3 = lax.broadcasted_iota(jnp.int32, (32, 4, CHORD), 1).astype(jnp.float32)
    lane3 = lax.broadcasted_iota(jnp.int32, (32, 4, CHORD), 2).astype(jnp.float32)
    belongs = (everything[:, 3:4, :] + row3 == lane3) & (row3 < 3.0)
    dots = jnp.sum(everything * amplitude, axis=2, keepdims=True)
    send3[1] = jnp.sum(jnp.sum(jnp.where(belongs, dots, 0.0), axis=0), axis=0, keepdims=True)
    share(1)
    counted = jnp.sum(jnp.where(lane3 == 62.0, everything, 0.0), axis=2, keepdims=True)
    counts = jnp.sum(jnp.sum(jnp.where(belongs, counted, 0.0), axis=0), axis=0, keepdims=True)
    counts = jnp.where(lane1 < BLADES, counts * CHORD, 1.0)

    arrived(recv3.at[0, pl.ds(0, 7)], recv_sem.at[5])
    amplitudes = jnp.concatenate([recv3[0, j] for j in range(8)], axis=0)
    both_parts = jnp.concatenate([amplitudes, pltpu.roll(amplitudes, 64, 1)], axis=0)
    both_parts = both_parts[:, 0:64].astype(jnp.bfloat16)
    for s in range(0, OWN, 4):
        lanes = slice(s * CHORD, (s + 4) * CHORD)
        rebuilt = jnp.dot(both_parts, shapes_flat[:, lanes], preferred_element_type=jnp.float32)
        product = jnp.sum(rebuilt * wall[:, lanes].astype(jnp.float32), axis=0, keepdims=True)
        for i in range(4):
            sens_ref[s + i : s + i + 1, :] = product[:, i * CHORD : (i + 1) * CHORD]

    arrived(recv3.at[1, pl.ds(0, 7)], recv_sem.at[6])
    totals = recv3[1, 0]
    for j in range(1, 8):
        totals = totals + recv3[1, j]
    load_ref[...] = totals * lax.rsqrt(counts)

    arrived(halves, send_sem.at[0])
    one_edge = first.at[pl.ds(0, 3), pl.ds(0, 3), pl.ds(0, HARM), :]
    arrived(one_edge, send_sem.at[1])
    arrived(one_edge, send_sem.at[2])
    arrived(recv1.at[pl.ds(0, 7)], send_sem.at[3])
    arrived(recv2.at[pl.ds(0, 31)], send_sem.at[4])
    arrived(recv3.at[0, pl.ds(0, 7)], send_sem.at[5])
    arrived(recv3.at[1, pl.ds(0, 7)], send_sem.at[6])


def per_device(source, mode_shapes, modal_real, modal_imag, harmonic_freq, blade_of_row):
    f32, bf16 = jnp.float32, jnp.bfloat16
    operands = (harmonic_freq, blade_of_row, source, mode_shapes, modal_real, modal_imag)
    hbm = pl.BlockSpec(memory_space=pltpu.HBM)
    vmem = pl.BlockSpec(memory_space=pltpu.VMEM)
    sens, load = pl.pallas_call(
        kernel,
        name="flutter",
        out_shape=(
            pltpu.VMEM((OWN, CHORD), f32),
            pltpu.VMEM((1, CHORD), f32),
        ),
        in_specs=[hbm] * 6,
        out_specs=(vmem, vmem),
        scratch_shapes=[
            pltpu.VMEM((MODES, OWN, CHORD), bf16),
            pltpu.VMEM((64 * OWN, CHORD), f32),
            pltpu.VMEM((64, OWN * CHORD), bf16),
            pltpu.VMEM((LAYERS, SPAN, 16, CHORD), f32),
            pltpu.VMEM((3, SPAN, 16, CHORD), f32),
            pltpu.VMEM((2, SPAN, 16, CHORD), f32),
            pltpu.VMEM((16, OWN * CHORD), bf16),
            pltpu.VMEM((16, OWN * CHORD), bf16),
            pltpu.VMEM((2, MODES, MODES), f32),
            pltpu.VMEM((CHORD, CHORD), f32),
            pltpu.VMEM((CHORD, CHORD), f32),
            pltpu.VMEM((32, CHORD), f32),
            pltpu.VMEM((8, 4, CHORD), f32),
            pltpu.VMEM((8, 4, CHORD), f32),
            pltpu.VMEM((4, CHORD), f32),
            pltpu.VMEM((32, 4, CHORD), f32),
            pltpu.VMEM((2, 1, CHORD), f32),
            pltpu.VMEM((2, 8, 1, CHORD), f32),
            pltpu.SMEM((HARM,), f32),
            pltpu.SMEM((2 * OWN,), jnp.int32),
            pltpu.SemaphoreType.DMA((6,)),
            pltpu.SemaphoreType.DMA((7,)),
            pltpu.SemaphoreType.DMA((7,)),
            pltpu.SemaphoreType.REGULAR((2,)),
        ],
        compiler_params=pltpu.CompilerParams(
            collective_id=0, has_side_effects=True, vmem_limit_bytes=32 * 1024 * 1024
        ),
    )(*(pltpu.with_memory_space_constraint(a, pltpu.HBM) for a in operands))
    return sens, load[0, :BLADES]


def solution(mesh):
    placed = (P("harm", None, "cells", None), P(None, "cells", None), P(), P(), P(), P("cells"))
    return jax.shard_map(
        per_device,
        mesh=mesh,
        in_specs=placed,
        out_specs=(P(("cells", "harm"), None), P()),
        check_vma=False,
    )
```

time: 37.1 us -> 30.8 us (0.83)
  Pallas kernels: 35.3 us -> 29 us
    pallas_call x1, Pallas kernels: 35.3 us -> 29 us  [per_device(): pl.pallas_call(kernel, name='flutter', out_shape=(pltpu.VMEM((OWN, CHORD)...]
where the time goes in v3:
time: 30.8 us
  Pallas kernels  29 us (94%)
  local copies, waits for them, and re-layouts  1.12 us (4%)
  between operations  0.64 us (2%)
    pallas_call x1, Pallas kernels, per_device(): pl.pallas_call(kernel, name='flutter', out_shape=(pltpu.VMEM((OWN, CHORD)...  29 us

profile of v3, /device:TPU:1, one launch (start us, length us, event | category | flops | bytes accessed | tf_op | source)
XLA Modules:
  0.0 30.8 jit_solution(7305979860734758644)
XLA Ops:
  0.6 29.0 %flutter.1 = (f32[32,128]{1,0:T(8,128)S(1)}, f32[1,128]{1,0:T(1,128)S(1)}) custom-call(f32[7]{0:T(128)} %freq_hbm.1, s32[64]{0:T(128)} %blade_hbm.1, f32[7,4,64,128]{3,2,1,0:T(8,128)} %source_ref.1, bf16[60,64,128]{2,1,0:T(8,128)(2,1)} %shapes_ref.1, f32[7,60,60]{2,1,0:T(8,128)} %real_ref.1, f32[7,60,60]{2,1,0:T(8,128)} %imag_ref.1), custom_call_target="tpu_custom_call" | custom-call | tf_op jit(solution)/shard_map/flutter/pallas_call | solution.py:395
  29.6 0.6 %copy.9 = f32[32,128]{1,0:T(8,128)} copy(f32[32,128]{1,0:T(8,128)S(1)} %get-tuple-element.6) | data formatting | bytes 32768
  30.2 0.5 %slice_bitcast_fusion = f32[24]{0:T(128)} fusion(f32[1,128]{1,0:T(1,128)S(1)} %get-tuple-element.5), kind=kLoop, calls=%fused_computation | loop fusion | bytes 192 | tf_op jit(solution)/shard_map/squeeze | solution.py:434

commit v4 on v3

v4 whole, which is shorter than its diff:
```python
import itertools

import jax
import jax.numpy as jnp
from jax import lax
from jax.experimental import pallas as pl
from jax.experimental.pallas import tpu as pltpu
from jax.sharding import PartitionSpec as P

BLADES = 24
RELAX = 0.15
DAMPING = 0.5
CENTER = 1.0 - 6.0 * RELAX - RELAX * DAMPING

HARM = 7
MODES = 60
LAYERS = 4
CHORD = 128
OWN = 32
EDGE_ROWS = ((0, 0), (1, 3), (2, 5))
PIVOTS = (8, 14)
SPAN = 38
XN, ZN, YN = 4, 8, 4
MESH = pl.DeviceIdType.MESH
HIGHEST = lax.Precision.HIGHEST


def place():
    cell = lax.axis_index("cells")
    return cell // (ZN * YN), (cell // YN) % ZN, cell % YN, lax.axis_index("harm")


def cell_of(x, z, y):
    return (x * ZN + z) * YN + y


def kernel(
    freq_hbm, blade_hbm, source_ref, shapes_ref, real_ref, imag_ref,
    sens_ref, load_ref,
    edge, edge_in, shapes_raw, shapes_wide, shapes_flat, first, second, third, wall,
    pair, gauss, inverse, packed, send1, recv1, send2, recv2, send3, recv3,
    freq_ref, blade_ref, local_sem, send_sem, recv_sem, known_sem,
):
    x, z, y, h = place()
    cell = lax.axis_index("cells")
    cells = XN * ZN * YN
    colour = lax.rem(x + 2 * y, 4)
    member = 4 * h + colour
    up_cell = lax.rem(cell + 1, cells)
    down_cell = lax.rem(cell + cells - 1, cells)
    mine = jnp.minimum(member, HARM - 1)

    barrier = pltpu.get_barrier_semaphore()

    def device(dx, dz, dy, dh=0):
        to_cell = cell_of(lax.rem(x + dx, XN), lax.rem(z + dz, ZN), lax.rem(y + dy, YN))
        return to_cell, lax.rem(h + dh, 2)

    def hops(step):
        return sum(min(d, n - d) for d, n in zip(step, (XN, ZN, YN)))

    chips = itertools.product(range(XN), range(ZN), range(YN))
    chips = sorted((c for c in chips if any(c)), key=lambda c: -hops(c))
    sources = [(1, 0, 0), (XN - 1, 0, 0), (0, 0, 1)]
    takers = [(XN - 1, 0, 0), (1, 0, 0), (0, 0, YN - 1)]
    takers = [(*c, dh) for c in takers for dh in range(2)] + [(0, 0, 0, 1)]
    near = [(0, 0, 0, 1)]
    near += [(*c, dh) for c in (*sources, (0, 0, YN - 1)) for dh in range(2)]
    near += [(2, 0, 0, 0), (0, 0, 2, 0)] + [(0, dz, 0, 0) for dz in (1, 2, ZN - 2, ZN - 1)]
    edge_cell = jnp.where(h == 0, down_cell, up_cell)
    nearby = [(edge_cell, 0), (edge_cell, 1)] + [device(*step) for step in near]
    for one in nearby:
        pl.semaphore_signal(barrier, inc=1, device_id=one, device_id_type=MESH)

    def arrived(array, sem):
        pltpu.make_async_copy(array, array, sem).wait()

    for c in range(HARM):
        for layer, offset in EDGE_ROWS:
            count = 3 - layer
            for side, station in ((0, 61 + layer), (1, 0)):
                pltpu.make_async_copy(
                    source_ref.at[c, layer, pl.ds(station, count), :],
                    edge.at[side, pl.ds(offset, count), c, :],
                    local_sem.at[6],
                ).start()
    freq_copy = pltpu.make_async_copy(freq_hbm, freq_ref, local_sem.at[4])
    blade_copy = pltpu.make_async_copy(blade_hbm, blade_ref, local_sem.at[5])
    freq_copy.start()
    blade_copy.start()
    pl.semaphore_wait(barrier, len(nearby))

    arrived(edge.at[:, :, pl.ds(0, HARM), :], local_sem.at[6])
    pltpu.make_async_remote_copy(
        src_ref=edge.at[0],
        dst_ref=edge_in.at[h],
        send_sem=send_sem.at[1],
        recv_sem=recv_sem.at[1],
        device_id=(up_cell, 0),
        device_id_type=MESH,
    ).start()
    pltpu.make_async_remote_copy(
        src_ref=edge.at[1],
        dst_ref=edge_in.at[h],
        send_sem=send_sem.at[2],
        recv_sem=recv_sem.at[1],
        device_id=(down_cell, 1),
        device_id_type=MESH,
    ).start()
    for c in range(HARM):
        pltpu.make_async_remote_copy(
            src_ref=source_ref.at[c, :, pl.ds((1 - h) * 29, 35), :],
            dst_ref=first.at[:, pl.ds(3 * h, 35), h * 8 + c, :],
            send_sem=send_sem.at[0],
            recv_sem=recv_sem.at[0],
            device_id=(cell, 1 - h),
            device_id_type=MESH,
        ).start()

    shape_copy = pltpu.make_async_copy(
        shapes_ref.at[:, pl.ds(pl.multiple_of(h * OWN, OWN), OWN), :],
        shapes_raw.at[pl.ds(0, MODES)],
        local_sem.at[1],
    )
    shape_copy.start()
    real_copy = pltpu.make_async_copy(real_ref.at[mine], pair.at[0], local_sem.at[2])
    imag_copy = pltpu.make_async_copy(imag_ref.at[mine], pair.at[1], local_sem.at[3])
    real_copy.start()
    imag_copy.start()
    start = h * 29
    for c in range(HARM):
        pltpu.make_async_copy(
            source_ref.at[c, :, pl.ds(start, 35), :],
            first.at[:, pl.ds(3 - 3 * h, 35), h * 8 + c, :],
            local_sem.at[0],
        ).start()
    blade_copy.wait()
    first_blade = blade_ref[0]
    last_blade = blade_ref[2 * OWN - 1]
    blade_row = h * OWN
    low_count = jnp.float32(0.0)
    for s in range(OWN):
        same = blade_ref[blade_row + s] == first_blade
        low_count = low_count + jnp.where(same, jnp.float32(1.0), jnp.float32(0.0))

    for step in [(0, 2, 0), (0, ZN - 2, 0), (1, 0, 0), (2, 0, 0), (3, 0, 0)]:
        pl.semaphore_signal(
            known_sem.at[0], inc=1, device_id=device(*step), device_id_type=MESH
        )

    shapes_wide[pl.ds(MODES * OWN, 4 * OWN), :] = jnp.zeros((4 * OWN, CHORD), jnp.float32)

    shape_copy.wait()

    def widen(m, carry):
        shapes_wide[pl.ds(pl.multiple_of(m * OWN, OWN), OWN), :] = shapes_raw[m].astype(jnp.float32)
        return carry

    lax.fori_loop(0, MODES, widen, 0, unroll=4)

    def flatten(s, carry):
        rows = shapes_wide[pl.ds(s, 64, stride=OWN), :]
        shapes_flat[:, pl.ds(pl.multiple_of(s * CHORD, CHORD), CHORD)] = rows.astype(jnp.bfloat16)
        return carry

    lax.fori_loop(0, OWN, flatten, 0, unroll=4)

    pl.semaphore_wait(known_sem.at[0], 5)
    flat = [c for c in chips if c[1] == 0]
    for step in flat:
        pl.semaphore_signal(
            known_sem.at[1], inc=1, device_id=device(*step), device_id_type=MESH
        )

    sub = lax.broadcasted_iota(jnp.int32, (16, CHORD), 0)
    lane16 = lax.broadcasted_iota(jnp.int32, (16, CHORD), 1)
    freq_copy.wait()
    coupling = jnp.zeros((16, CHORD), jnp.float32)
    for k in range(HARM):
        value = RELAX * freq_ref[k]
        coupling = jnp.where(sub == k, value, jnp.where(sub == 8 + k, -value, coupling))
    not_last = lane16 < CHORD - 1
    not_first = lane16 > 0

    def relaxed(field, layers, layer, t):
        centre = field[layer, t]
        near = field[layer, t + 1] + field[layer, t - 1]
        near = near + jnp.where(not_last, pltpu.roll(centre, CHORD - 1, 1), 0.0)
        near = near + jnp.where(not_first, pltpu.roll(centre, 1, 1), 0.0)
        if layer + 1 < layers:
            near = near + field[layer + 1, t]
        if layer > 0:
            near = near + field[layer - 1, t]
        partner = jnp.concatenate([centre[8:16], centre[0:8]], axis=0)
        return CENTER * centre + coupling * partner + RELAX * (near + first[layer, t])

    in_use = (sub != 7) & (sub != 15)

    def relax_rows(first_t, second_t, third_t, first_n, second_n, third_n):
        def step_one(i, carry):
            for layer in range(3):
                second[layer, first_t + i] = relaxed(first, 4, layer, first_t + i)
            return carry

        def step_two(i, carry):
            for layer in range(2):
                third[layer, second_t + i] = relaxed(second, 3, layer, second_t + i)
            return carry

        def step_three(i, carry):
            s = third_t - 3 + i
            value = jnp.where(in_use, relaxed(third, 2, 0, third_t + i), 0.0).astype(jnp.bfloat16)
            same = blade_ref[blade_row + s] == first_blade
            weight = jnp.where(same, jnp.float32(1.0), jnp.float32(0.0))
            lanes = pl.ds(pl.multiple_of(s * CHORD, CHORD), CHORD)
            wall[0:16, lanes] = value
            wall[16:32, lanes] = (value.astype(jnp.float32) * weight).astype(jnp.bfloat16)
            return carry

        lax.fori_loop(0, first_n, step_one, 0, unroll=min(first_n, 11))
        lax.fori_loop(0, second_n, step_two, 0, unroll=min(second_n, 16))
        lax.fori_loop(0, third_n, step_three, 0, unroll=True)

    contract = (((1,), (1,)), ((), ()))

    def loads(lanes):
        packed[:, 0:64] += lax.dot_general(
            wall[:, lanes], shapes_flat[:, lanes], contract, preferred_element_type=jnp.float32
        )

    edge_lanes = pl.ds(pl.multiple_of(h * (29 * CHORD), CHORD), 3 * CHORD)
    wall[:, edge_lanes] = jnp.zeros((32, 3 * CHORD), jnp.bfloat16)
    packed[...] = jnp.zeros_like(packed)
    halves = first.at[:, pl.ds(0, 35), pl.ds(0, HARM), :]
    arrived(halves, local_sem.at[0])
    arrived(halves, recv_sem.at[0])
    relax_rows(4 - 3 * h, 4 - 2 * h, 6 - 3 * h, 33, 32, 29)
    loads(pl.ds(0, OWN * CHORD))
    lane = lax.broadcasted_iota(jnp.int32, (64, CHORD), 1)
    left_half = lane < 64
    real_copy.wait()
    imag_copy.wait()
    gauss[...] = jnp.zeros_like(gauss)
    gauss[0:MODES, 0:MODES] = pair[0]
    gauss[64 : 64 + MODES, 0:MODES] = pair[1]
    both = gauss[0:64, :] + pltpu.roll(gauss[64:128, :], 64, 1)
    system = jnp.concatenate([both, jnp.zeros_like(both)], axis=0)
    adjoint = jnp.transpose(system)
    gram = jnp.dot(adjoint, system, precision=HIGHEST, preferred_element_type=jnp.float32)
    top, low = gram[0:64], gram[64:128]
    gauss[0:64, :] = jnp.where(
        left_half, top + pltpu.roll(low, 64, 1), pltpu.roll(adjoint[0:64], 64, 1)
    )
    gauss[64:128, :] = jnp.where(
        left_half, pltpu.roll(top, 64, 1) - low, -pltpu.roll(adjoint[64:128], 64, 1)
    )

    def pivot(k, carry):
        pick = jnp.full((8, CHORD), k, jnp.int32)
        row_re = jnp.broadcast_to(gauss[pl.ds(k, 1), :], (8, CHORD))
        row_im = jnp.broadcast_to(gauss[pl.ds(64 + k, 1), :], (8, CHORD))
        scale = 1.0 / jnp.take_along_axis(row_re, pick, axis=1)
        row_re = row_re * scale
        row_im = row_im * scale
        for block in range(8):
            here, there = pl.ds(8 * block, 8), pl.ds(64 + 8 * block, 8)
            old_re, old_im = gauss[here, :], gauss[there, :]
            col_re = jnp.take_along_axis(old_re, pick, axis=1)
            col_im = jnp.take_along_axis(old_im, pick, axis=1)
            gauss[here, :] = old_re - col_re * row_re + col_im * row_im
            gauss[there, :] = old_im - col_re * row_im - col_im * row_re
        gauss[pl.ds(k, 1), :] = row_re[0:1]
        gauss[pl.ds(64 + k, 1), :] = row_im[0:1]
        return carry

    lax.fori_loop(0, PIVOTS[0], pivot, 0)
    arrived(edge_in, recv_sem.at[1])
    for core in range(2):
        for layer, offset in EDGE_ROWS:
            for i in range(3 - layer):
                t = i + layer * (1 - h) + 35 * h
                first[layer, t, 8 * core : 8 * core + 8, :] = edge_in[core, offset + i]
    relax_rows(1 + 33 * h, 2 + 31 * h, 3 + 29 * h, 3, 3, 3)
    loads(edge_lanes)

    lane8 = lax.broadcasted_iota(jnp.int32, (8, CHORD), 1)
    whole = packed[0:8, :] + pltpu.roll(packed[8:16, :], 64, 1)
    lower = packed[16:24, :] + pltpu.roll(packed[24:32, :], 64, 1)
    upper = whole - lower
    lower = jnp.where(lane8 == 62, low_count, lower)
    upper = jnp.where(lane8 == 62, OWN - low_count, upper)
    for core in range(2):
        send1[core, 0:4, :] = lower[4 * core : 4 * core + 4]
        send1[core, 4:8, :] = upper[4 * core : 4 * core + 4]
    pltpu.make_async_remote_copy(
        src_ref=send1.at[1 - h],
        dst_ref=recv1,
        send_sem=send_sem.at[3],
        recv_sem=recv_sem.at[3],
        device_id=(cell, 1 - h),
        device_id_type=MESH,
    ).start()

    lax.fori_loop(PIVOTS[0], PIVOTS[1], pivot, 0)
    arrived(recv1, recv_sem.at[3])

    lane1 = lax.broadcasted_iota(jnp.int32, (1, CHORD), 1)
    low_id = jnp.full((1, CHORD), first_blade, jnp.int32).astype(jnp.float32)
    high_id = jnp.full((1, CHORD), last_blade, jnp.int32).astype(jnp.float32)
    chip_rows = send1[h] + recv1[...]
    send2[0] = jnp.where(lane1 == 63, low_id, chip_rows[0:4])
    send2[1] = jnp.where(lane1 == 63, high_id, chip_rows[4:8])
    two_rows = pl.ds(2 * cell, 2)
    recv2[pl.ds(2 * cell, 1), :] = send2[0, pl.ds(colour, 1), :]
    recv2[pl.ds(2 * cell + 1, 1), :] = send2[1, pl.ds(colour, 1), :]
    pl.semaphore_wait(known_sem.at[1], len(flat))
    for step in chips:
        pltpu.make_async_remote_copy(
            src_ref=send2.at[:, lax.rem(colour + step[0] + 2 * step[2], 4), :],
            dst_ref=recv2.at[two_rows],
            send_sem=send_sem.at[4],
            recv_sem=recv_sem.at[4],
            device_id=device(*step),
            device_id_type=MESH,
        ).start()

    lax.fori_loop(PIVOTS[1], MODES, pivot, 0)
    back_re = pltpu.roll(gauss[0:64, :], 64, 1)
    back_im = pltpu.roll(gauss[64:128, :], 64, 1)
    inverse[0:64, :] = jnp.where(left_half, back_re, -gauss[64:128, :])
    inverse[64:128, :] = jnp.where(left_half, back_im, gauss[0:64, :])

    arrived(recv2.at[pl.ds(0, 254)], recv_sem.at[4])
    everything = recv2[...]
    total = jnp.sum(everything, axis=0, keepdims=True)
    used = (lane1 < MODES) | ((lane1 >= 64) & (lane1 < 64 + MODES))
    total = jnp.where(used, total * (1.0 / 1024.0), 0.0)
    solved = lax.dot_general(
        jnp.broadcast_to(total, (8, CHORD)), inverse[...], contract,
        precision=HIGHEST, preferred_element_type=jnp.float32,
    )[0:1]
    amplitude = jnp.where(used, solved, 0.0).astype(jnp.bfloat16).astype(jnp.float32)

    def share(part):
        recv3[part, pl.ds(member, 1), :] = send3[part]
        for step in takers:
            pltpu.make_async_remote_copy(
                src_ref=send3.at[part],
                dst_ref=recv3.at[part, pl.ds(member, 1)],
                send_sem=send_sem.at[5 + part],
                recv_sem=recv_sem.at[5 + part],
                device_id=device(*step),
                device_id_type=MESH,
            ).start()

    send3[0] = amplitude
    share(0)
    lane2 = lax.broadcasted_iota(jnp.int32, (256, CHORD), 1).astype(jnp.float32)

    def along(values):
        return jnp.sum(values, axis=1, keepdims=True)

    belongs = along(jnp.where(lane2 == 63.0, everything, 0.0)) == lane2

    def by_blade(values):
        return jnp.sum(jnp.where(belongs, values, 0.0), axis=0, keepdims=True)

    send3[1] = by_blade(along(everything * amplitude))
    share(1)
    counts = by_blade(along(jnp.where(lane2 == 62.0, everything, 0.0)))
    counts = jnp.where(lane1 < BLADES, counts * CHORD, 1.0)

    arrived(recv3.at[0, pl.ds(0, 7)], recv_sem.at[5])
    amplitudes = recv3[0]
    both_parts = jnp.concatenate([amplitudes, pltpu.roll(amplitudes, 64, 1)], axis=0)
    both_parts = both_parts[:, 0:64].astype(jnp.bfloat16)
    for s in range(0, OWN, 4):
        lanes = slice(s * CHORD, (s + 4) * CHORD)
        rebuilt = jnp.dot(both_parts, shapes_flat[:, lanes], preferred_element_type=jnp.float32)
        product = jnp.sum(rebuilt * wall[0:16, lanes].astype(jnp.float32), axis=0, keepdims=True)
        for i in range(4):
            sens_ref[s + i : s + i + 1, :] = product[:, i * CHORD : (i + 1) * CHORD]

    arrived(recv3.at[1, pl.ds(0, 7)], recv_sem.at[6])
    totals = jnp.sum(recv3[1], axis=0, keepdims=True)
    load_ref[...] = totals * lax.rsqrt(counts)

    arrived(halves, send_sem.at[0])
    arrived(edge.at[0], send_sem.at[1])
    arrived(edge.at[1], send_sem.at[2])
    arrived(recv1, send_sem.at[3])
    arrived(recv2.at[pl.ds(0, 254)], send_sem.at[4])
    arrived(recv3.at[0, pl.ds(0, 7)], send_sem.at[5])
    arrived(recv3.at[1, pl.ds(0, 7)], send_sem.at[6])


def per_device(source, mode_shapes, modal_real, modal_imag, harmonic_freq, blade_of_row):
    f32, bf16 = jnp.float32, jnp.bfloat16
    operands = (harmonic_freq, blade_of_row, source, mode_shapes, modal_real, modal_imag)
    hbm = pl.BlockSpec(memory_space=pltpu.HBM)
    vmem = pl.BlockSpec(memory_space=pltpu.VMEM)
    sens, load = pl.pallas_call(
        kernel,
        name="flutter",
        out_shape=(
            pltpu.VMEM((OWN, CHORD), f32),
            pltpu.VMEM((1, CHORD), f32),
        ),
        in_specs=[hbm] * 6,
        out_specs=(vmem, vmem),
        scratch_shapes=[
            pltpu.VMEM((2, 6, 8, CHORD), f32),
            pltpu.VMEM((2, 6, 8, CHORD), f32),
            pltpu.VMEM((MODES, OWN, CHORD), bf16),
            pltpu.VMEM((64 * OWN, CHORD), f32),
            pltpu.VMEM((64, OWN * CHORD), bf16),
            pltpu.VMEM((LAYERS, SPAN, 16, CHORD), f32),
            pltpu.VMEM((3, SPAN, 16, CHORD), f32),
            pltpu.VMEM((2, SPAN, 16, CHORD), f32),
            pltpu.VMEM((32, OWN * CHORD), bf16),
            pltpu.VMEM((2, MODES, MODES), f32),
            pltpu.VMEM((CHORD, CHORD), f32),
            pltpu.VMEM((CHORD, CHORD), f32),
            pltpu.VMEM((32, CHORD), f32),
            pltpu.VMEM((2, 8, CHORD), f32),
            pltpu.VMEM((8, CHORD), f32),
            pltpu.VMEM((2, 4, CHORD), f32),
            pltpu.VMEM((256, CHORD), f32),
            pltpu.VMEM((2, 1, CHORD), f32),
            pltpu.VMEM((2, 8, CHORD), f32),
            pltpu.SMEM((HARM,), f32),
            pltpu.SMEM((2 * OWN,), jnp.int32),
            pltpu.SemaphoreType.DMA((7,)),
            pltpu.SemaphoreType.DMA((7,)),
            pltpu.SemaphoreType.DMA((7,)),
            pltpu.SemaphoreType.REGULAR((2,)),
        ],
        compiler_params=pltpu.CompilerParams(
            collective_id=0, has_side_effects=True, vmem_limit_bytes=32 * 1024 * 1024
        ),
    )(*(pltpu.with_memory_space_constraint(a, pltpu.HBM) for a in operands))
    return sens, load[0, :BLADES]


def solution(mesh):
    placed = (P("harm", None, "cells", None), P(None, "cells", None), P(), P(), P(), P("cells"))
    return jax.shard_map(
        per_device,
        mesh=mesh,
        in_specs=placed,
        out_specs=(P(("cells", "harm"), None), P()),
        check_vma=False,
    )
```

time: 30.8 us -> 29.8 us (0.968)
  Pallas kernels: 29 us -> 27.9 us
    pallas_call x1, Pallas kernels: 29 us -> 27.9 us  [per_device(): pl.pallas_call(kernel, name='flutter', out_shape=(pltpu.VMEM((OWN, CHORD)...]
where the time goes in v4:
time: 29.8 us; the launch traced here: 29.7 us
  Pallas kernels  27.9 us (94%)
  local copies, waits for them, and re-layouts  1.12 us (4%)
  between operations  0.64 us (2%)
    pallas_call x1, Pallas kernels, per_device(): pl.pallas_call(kernel, name='flutter', out_shape=(pltpu.VMEM((OWN, CHORD)...  27.9 us
    unnamed x1, local copies, waits for them, and re-layouts  0.61 us

profile of v4, /device:TPU:1, one launch (start us, length us, event | category | flops | bytes accessed | tf_op | source)
XLA Modules:
  0.0 29.7 jit_solution(10616571784890176631)
XLA Ops:
  0.6 27.9 %flutter.1 = (f32[32,128]{1,0:T(8,128)S(1)}, f32[1,128]{1,0:T(1,128)S(1)}) custom-call(f32[7]{0:T(128)} %freq_hbm.1, s32[64]{0:T(128)} %blade_hbm.1, f32[7,4,64,128]{3,2,1,0:T(8,128)} %source_ref.1, bf16[60,64,128]{2,1,0:T(8,128)(2,1)} %shapes_ref.1, f32[7,60,60]{2,1,0:T(8,128)} %real_ref.1, f32[7,60,60]{2,1,0:T(8,128)} %imag_ref.1), custom_call_target="tpu_custom_call" | custom-call | tf_op jit(solution)/shard_map/flutter/pallas_call | solution.py:402
  28.5 0.6 %copy.9 = f32[32,128]{1,0:T(8,128)} copy(f32[32,128]{1,0:T(8,128)S(1)} %get-tuple-element.6) | data formatting | bytes 32768
  29.2 0.5 %slice_bitcast_fusion = f32[24]{0:T(128)} fusion(f32[1,128]{1,0:T(1,128)S(1)} %get-tuple-element.5), kind=kLoop, calls=%fused_computation | loop fusion | bytes 192 | tf_op jit(solution)/shard_map/squeeze | solution.py:442

commit v5 on v4

--- a/solution.py
+++ b/solution.py
@@ -18,7 +18,6 @@
 CHORD = 128
 OWN = 32
 EDGE_ROWS = ((0, 0), (1, 3), (2, 5))
-PIVOTS = (8, 14)
 SPAN = 38
 XN, ZN, YN = 4, 8, 4
 MESH = pl.DeviceIdType.MESH
@@ -236,44 +235,6 @@
     arrived(halves, recv_sem.at[0])
     relax_rows(4 - 3 * h, 4 - 2 * h, 6 - 3 * h, 33, 32, 29)
     loads(pl.ds(0, OWN * CHORD))
-    lane = lax.broadcasted_iota(jnp.int32, (64, CHORD), 1)
-    left_half = lane < 64
-    real_copy.wait()
-    imag_copy.wait()
-    gauss[...] = jnp.zeros_like(gauss)
-    gauss[0:MODES, 0:MODES] = pair[0]
-    gauss[64 : 64 + MODES, 0:MODES] = pair[1]
-    both = gauss[0:64, :] + pltpu.roll(gauss[64:128, :], 64, 1)
-    system = jnp.concatenate([both, jnp.zeros_like(both)], axis=0)
-    adjoint = jnp.transpose(system)
-    gram = jnp.dot(adjoint, system, precision=HIGHEST, preferred_element_type=jnp.float32)
-    top, low = gram[0:64], gram[64:128]
-    gauss[0:64, :] = jnp.where(
-        left_half, top + pltpu.roll(low, 64, 1), pltpu.roll(adjoint[0:64], 64, 1)
-    )
-    gauss[64:128, :] = jnp.where(
-        left_half, pltpu.roll(top, 64, 1) - low, -pltpu.roll(adjoint[64:128], 64, 1)
-    )
-
-    def pivot(k, carry):
-        pick = jnp.full((8, CHORD), k, jnp.int32)
-        row_re = jnp.broadcast_to(gauss[pl.ds(k, 1), :], (8, CHORD))
-        row_im = jnp.broadcast_to(gauss[pl.ds(64 + k, 1), :], (8, CHORD))
-        scale = 1.0 / jnp.take_along_axis(row_re, pick, axis=1)
-        row_re = row_re * scale
-        row_im = row_im * scale
-        for block in range(8):
-            here, there = pl.ds(8 * block, 8), pl.ds(64 + 8 * block, 8)
-            old_re, old_im = gauss[here, :], gauss[there, :]
-            col_re = jnp.take_along_axis(old_re, pick, axis=1)
-            col_im = jnp.take_along_axis(old_im, pick, axis=1)
-            gauss[here, :] = old_re - col_re * row_re + col_im * row_im
-            gauss[there, :] = old_im - col_re * row_im - col_im * row_re
-        gauss[pl.ds(k, 1), :] = row_re[0:1]
-        gauss[pl.ds(64 + k, 1), :] = row_im[0:1]
-        return carry
-
-    lax.fori_loop(0, PIVOTS[0], pivot, 0)
     arrived(edge_in, recv_sem.at[1])
     for core in range(2):
         for layer, offset in EDGE_ROWS:
@@ -301,7 +262,6 @@
         device_id_type=MESH,
     ).start()
 
-    lax.fori_loop(PIVOTS[0], PIVOTS[1], pivot, 0)
     arrived(recv1, recv_sem.at[3])
 
     lane1 = lax.broadcasted_iota(jnp.int32, (1, CHORD), 1)
@@ -324,7 +284,44 @@
             device_id_type=MESH,
         ).start()
 
-    lax.fori_loop(PIVOTS[1], MODES, pivot, 0)
+    lane = lax.broadcasted_iota(jnp.int32, (64, CHORD), 1)
+    left_half = lane < 64
+    real_copy.wait()
+    imag_copy.wait()
+    gauss[...] = jnp.zeros_like(gauss)
+    gauss[0:MODES, 0:MODES] = pair[0]
+    gauss[64 : 64 + MODES, 0:MODES] = pair[1]
+    both = gauss[0:64, :] + pltpu.roll(gauss[64:128, :], 64, 1)
+    system = jnp.concatenate([both, jnp.zeros_like(both)], axis=0)
+    adjoint = jnp.transpose(system)
+    gram = jnp.dot(adjoint, system, precision=HIGHEST, preferred_element_type=jnp.float32)
+    top, low = gram[0:64], gram[64:128]
+    gauss[0:64, :] = jnp.where(
+        left_half, top + pltpu.roll(low, 64, 1), pltpu.roll(adjoint[0:64], 64, 1)
+    )
+    gauss[64:128, :] = jnp.where(
+        left_half, pltpu.roll(top, 64, 1) - low, -pltpu.roll(adjoint[64:128], 64, 1)
+    )
+
+    def pivot(k, carry):
+        pick = jnp.full((8, CHORD), k, jnp.int32)
+        row_re = jnp.broadcast_to(gauss[pl.ds(k, 1), :], (8, CHORD))
+        row_im = jnp.broadcast_to(gauss[pl.ds(64 + k, 1), :], (8, CHORD))
+        scale = 1.0 / jnp.take_along_axis(row_re, pick, axis=1)
+        row_re = row_re * scale
+        row_im = row_im * scale
+        for block in range(8):
+            here, there = pl.ds(8 * block, 8), pl.ds(64 + 8 * block, 8)
+            old_re, old_im = gauss[here, :], gauss[there, :]
+            col_re = jnp.take_along_axis(old_re, pick, axis=1)
+            col_im = jnp.take_along_axis(old_im, pick, axis=1)
+            gauss[here, :] = old_re - col_re * row_re + col_im * row_im
+            gauss[there, :] = old_im - col_re * row_im - col_im * row_re
+        gauss[pl.ds(k, 1), :] = row_re[0:1]
+        gauss[pl.ds(64 + k, 1), :] = row_im[0:1]
+        return carry
+
+    lax.fori_loop(0, MODES, pivot, 0)
     back_re = pltpu.roll(gauss[0:64, :], 64, 1)
     back_im = pltpu.roll(gauss[64:128, :], 64, 1)
     inverse[0:64, :] = jnp.where(left_half, back_re, -gauss[64:128, :])

time: 29.8 us -> 28.5 us (0.956)
  Pallas kernels: 27.9 us -> 26.7 us
    pallas_call x1, Pallas kernels: 27.9 us -> 26.7 us  [per_device(): pl.pallas_call(kernel, name='flutter', out_shape=(pltpu.VMEM((OWN, CHORD)...]
where the time goes in v5:
time: 28.5 us; the launch traced here: 28.4 us
  Pallas kernels  26.7 us (94%)
  local copies, waits for them, and re-layouts  1.12 us (4%)
  between operations  0.64 us (2%)
    pallas_call x1, Pallas kernels, per_device(): pl.pallas_call(kernel, name='flutter', out_shape=(pltpu.VMEM((OWN, CHORD)...  26.7 us
    unnamed x1, local copies, waits for them, and re-layouts  0.61 us

profile of v5, /device:TPU:1, one launch (start us, length us, event | category | flops | bytes accessed | tf_op | source)
XLA Modules:
  0.0 28.4 jit_solution(3227298178651752624)
XLA Ops:
  0.6 26.7 %flutter.1 = (f32[32,128]{1,0:T(8,128)S(1)}, f32[1,128]{1,0:T(1,128)S(1)}) custom-call(f32[7]{0:T(128)} %freq_hbm.1, s32[64]{0:T(128)} %blade_hbm.1, f32[7,4,64,128]{3,2,1,0:T(8,128)} %source_ref.1, bf16[60,64,128]{2,1,0:T(8,128)(2,1)} %shapes_ref.1, f32[7,60,60]{2,1,0:T(8,128)} %real_ref.1, f32[7,60,60]{2,1,0:T(8,128)} %imag_ref.1), custom_call_target="tpu_custom_call" | custom-call | tf_op jit(solution)/shard_map/flutter/pallas_call | solution.py:399
  27.3 0.6 %copy.9 = f32[32,128]{1,0:T(8,128)} copy(f32[32,128]{1,0:T(8,128)S(1)} %get-tuple-element.6) | data formatting | bytes 32768
  27.9 0.5 %slice_bitcast_fusion = f32[24]{0:T(128)} fusion(f32[1,128]{1,0:T(1,128)S(1)} %get-tuple-element.5), kind=kLoop, calls=%fused_computation | loop fusion | bytes 192 | tf_op jit(solution)/shard_map/squeeze | solution.py:439

commit v6 on v5

--- a/solution.py
+++ b/solution.py
@@ -216,8 +216,9 @@
             wall[16:32, lanes] = (value.astype(jnp.float32) * weight).astype(jnp.bfloat16)
             return carry
 
-        lax.fori_loop(0, first_n, step_one, 0, unroll=min(first_n, 11))
-        lax.fori_loop(0, second_n, step_two, 0, unroll=min(second_n, 16))
+        if first_n:
+            lax.fori_loop(0, first_n, step_one, 0, unroll=min(first_n, 11))
+            lax.fori_loop(0, second_n, step_two, 0, unroll=min(second_n, 16))
         lax.fori_loop(0, third_n, step_three, 0, unroll=True)
 
     contract = (((1,), (1,)), ((), ()))
@@ -241,7 +242,15 @@
             for i in range(3 - layer):
                 t = i + layer * (1 - h) + 35 * h
                 first[layer, t, 8 * core : 8 * core + 8, :] = edge_in[core, offset + i]
-    relax_rows(1 + 33 * h, 2 + 31 * h, 3 + 29 * h, 3, 3, 3)
+    for layer, steps in ((0, (1, 2, 3)), (1, (2, 3)), (2, (3,))):
+        for step in steps:
+            t = step + h * (SPAN - 1 - 2 * step)
+            second[layer, t] = relaxed(first, 4, layer, t)
+    for layer, steps in ((0, (2, 3, 4)), (1, (3, 4))):
+        for step in steps:
+            t = step + h * (SPAN - 1 - 2 * step)
+            third[layer, t] = relaxed(second, 3, layer, t)
+    relax_rows(0, 0, 3 + 29 * h, 0, 0, 3)
     loads(edge_lanes)
 
     lane8 = lax.broadcasted_iota(jnp.int32, (8, CHORD), 1)

time: 28.5 us -> 28.5 us (level)
  no operation moved by 1% of the time
where the time goes in v6:
time: 28.5 us; the launch traced here: 28.4 us
  Pallas kernels  26.6 us (93%)
  local copies, waits for them, and re-layouts  1.12 us (4%)
  between operations  0.64 us (2%)
    pallas_call x1, Pallas kernels, per_device(): pl.pallas_call(kernel, name='flutter', out_shape=(pltpu.VMEM((OWN, CHORD)...  26.6 us
    unnamed x1, local copies, waits for them, and re-layouts  0.61 us

profile of v6, /device:TPU:1, one launch (start us, length us, event | category | flops | bytes accessed | tf_op | source)
XLA Modules:
  0.0 28.4 jit_solution(1037394364018471919)
XLA Ops:
  0.6 26.6 %flutter.1 = (f32[32,128]{1,0:T(8,128)S(1)}, f32[1,128]{1,0:T(1,128)S(1)}) custom-call(f32[7]{0:T(128)} %freq_hbm.1, s32[64]{0:T(128)} %blade_hbm.1, f32[7,4,64,128]{3,2,1,0:T(8,128)} %source_ref.1, bf16[60,64,128]{2,1,0:T(8,128)(2,1)} %shapes_ref.1, f32[7,60,60]{2,1,0:T(8,128)} %real_ref.1, f32[7,60,60]{2,1,0:T(8,128)} %imag_ref.1), custom_call_target="tpu_custom_call" | custom-call | tf_op jit(solution)/shard_map/flutter/pallas_call | solution.py:408
  27.3 0.6 %copy.9 = f32[32,128]{1,0:T(8,128)} copy(f32[32,128]{1,0:T(8,128)S(1)} %get-tuple-element.6) | data formatting | bytes 32768
  27.9 0.5 %slice_bitcast_fusion = f32[24]{0:T(128)} fusion(f32[1,128]{1,0:T(1,128)S(1)} %get-tuple-element.5), kind=kLoop, calls=%fused_computation | loop fusion | bytes 192 | tf_op jit(solution)/shard_map/squeeze | solution.py:448
